TPU v7x, 256 devices: a whole 4x4x8 slice. The times are simulated.
256 devices in a mesh: segment: 32 (over x, z_lo, y), tp: 8 (over z_hi, core).
Axes of the slice: x: 4, y: 4, z: 8 (z_hi: 4, z_lo: 2; z = z_hi * 2 + z_lo), core: 2. Of those that a mesh axis runs over, the one named last changes fastest.
Arguments:
- partials: bfloat16 [32, 8, 256, 4096], P('segment', 'tp'), may hold values from -6 to 6
- residual: bfloat16 [32, 256, 4096], P('segment', 'tp'), may hold values from -80 to 80
- norm_gain: float32 [32, 4096], P('segment'), may hold values from 0.1 to 1.9
- w_query: bfloat16 [32, 4096, 8, 8, 128], P('segment', None, 'tp'), may hold values from -12 to 12
- w_keyval: bfloat16 [32, 4096, 8, 2, 128], P('segment', None, 'tp'), may hold values from -1 to 1
Outputs:
- attended: bfloat16 [32, 256, 8, 8, 128], P('segment', None, 'tp')
All inputs are finite; a program needn't handle non-finite values.
Results may differ from a plain program's by a relative error of at most 0.03.
Values may be sent and summed in bfloat16 or wider, within the bound.
No kernel may reach another device: no remote copies, remote signals or barrier semaphores. Data moves between devices by JAX's collectives and lax.ppermute only.
A program may use at most 128 MiB of HBM per device.

v0:
```python
import math

import jax
import jax.numpy as jnp
from jax import lax
from jax.sharding import PartitionSpec as P

ROPE_BASE = 500000.0
NORM_EPS = 1e-05


def from_behind(value, axis, steps):
    count = lax.axis_size(axis)
    pairs = [(source, (source + steps) % count) for source in range(count)]
    return lax.ppermute(value, axis, pairs)


def rotate(stacked, positions):
    half_dim = stacked.shape[-1] // 2
    frequency = ROPE_BASE ** (-jnp.arange(half_dim, dtype=jnp.float32) * 2.0 / stacked.shape[-1])
    angles = positions[:, None] * frequency[None, :]
    angles = angles.reshape((stacked.shape[0],) + (1,) * (stacked.ndim - 2) + (half_dim,))
    cosine = jnp.cos(angles)
    sine_part = jnp.sin(angles)
    first_half = stacked[..., :half_dim]
    second_half = stacked[..., half_dim:]
    return jnp.concatenate(
        [
            first_half * cosine - second_half * sine_part,
            second_half * cosine + first_half * sine_part,
        ],
        axis=-1,
    )


def per_device(partials, residual, norm_gain, w_query, w_keyval):
    token_count = partials.shape[2]
    model_width = partials.shape[3]
    kv_dev = w_query.shape[2]
    group_size = w_query.shape[3]
    head_dim = w_query.shape[4]
    query_matrix = w_query[0].reshape(model_width, -1)
    keyval_matrix = w_keyval[0].reshape(model_width, -1)
    gain_row = norm_gain[0]
    local_term = partials[0, 0].astype(jnp.float32)
    summed = lax.psum(local_term.astype(jnp.bfloat16), "tp").astype(jnp.float32)
    residual_full = lax.all_gather(residual[0], "tp", axis=0, tiled=True)
    made = (summed + residual_full.astype(jnp.float32)).astype(jnp.bfloat16)
    received = from_behind(made, "segment", 1)
    values_f = received.astype(jnp.float32)
    mean_sq = jnp.mean(values_f * values_f, axis=-1, keepdims=True)
    normed = (values_f * lax.rsqrt(mean_sq + NORM_EPS) * gain_row[None, :]).astype(jnp.bfloat16)
    queries = jnp.dot(normed, query_matrix, preferred_element_type=jnp.float32)
    key_value = jnp.dot(normed, keyval_matrix, preferred_element_type=jnp.float32)
    mixed = jnp.concatenate([queries, key_value], axis=1)
    query_cols = kv_dev * group_size * head_dim
    queries = mixed[:, :query_cols].reshape(token_count, kv_dev, group_size, head_dim)
    key_value = mixed[:, query_cols:].reshape(token_count, kv_dev, 2, head_dim)
    positions = jnp.arange(token_count).astype(jnp.float32)
    queries = rotate(queries, positions).astype(jnp.bfloat16)
    keys_rot = rotate(key_value[:, :, 0], positions).astype(jnp.bfloat16)
    values = key_value[:, :, 1].astype(jnp.bfloat16)
    scores = jnp.einsum(
        "tkgd,skd->kgts", queries, keys_rot, preferred_element_type=jnp.float32
    ) / math.sqrt(head_dim)
    index_row = jnp.arange(token_count)
    causal = index_row[:, None] >= index_row[None, :]
    scores = jnp.where(causal[None, None], scores, -jnp.inf)
    attn_weights = jax.nn.softmax(scores, axis=-1).astype(jnp.bfloat16)
    attended = jnp.einsum(
        "kgts,skd->tkgd", attn_weights, values, preferred_element_type=jnp.float32
    )
    return attended.astype(jnp.bfloat16)[None]


def solution(mesh):
    placed = (
        P("segment", "tp", None, None),
        P("segment", "tp", None),
        P("segment", None),
        P("segment", None, "tp", None, None),
        P("segment", None, "tp", None, None),
    )
    return jax.shard_map(
        per_device,
        mesh=mesh,
        in_specs=placed,
        out_specs=P("segment", None, "tp", None, None),
        check_vma=False,
    )
```

profile of v0, /device:TPU:1, one launch (start us, length us, event | category | flops | bytes accessed | tf_op | source)
XLA Modules:
  0.0 211.8 jit_solution(5135222394739233132)
XLA Ops:
  6.5 0.0 all-reduce.2.cloned.1.call-start
  6.5 0.7 all-reduce.2.cloned.1.call-update
  7.3 0.0 all-gather.3.cloned.1.call-start
  7.3 0.7 all-gather.3.cloned.1.call-update
  8.0 89.2 %all-reduce.2.cloned.1.call-done = bf16[256,4096]{1,0:T(8,128)(2,1)} async-done(((bf16[256,4096]{1,0:T(8,128)(2,1)}), bf16[256,4096]{1,0:T(8,128)(2,1)}) %all-reduce.2.cloned.1.call-update) | async-done | bytes 2097168 | tf_op jit(solution)/shard_map/psum | solution.py:46
  97.2 39.2 %all-gather.3.cloned.1.call-done = bf16[1,256,4096]{2,1,0:T(8,128)(2,1)} async-done(((bf16[1,32,4096]{2,1,0:T(8,128)(2,1)}), bf16[1,256,4096]{2,1,0:T(8,128)(2,1)}) %all-gather.3.cloned.1.call-update) | async-done | bytes 2097168 | tf_op jit(solution)/shard_map/all_gather | solution.py:47
  136.4 4.3 %fusion.3 = bf16[256,4096]{1,0:T(8,128)(2,1)} fusion(bf16[256,4096]{1,0:T(8,128)(2,1)} %all-reduce.2.cloned.1.call-done, bf16[1,256,4096]{2,1,0:T(8,128)(2,1)} %all-gather.3.cloned.1.call-done), kind=kLoop, calls=%fused_computation.7 | loop fusion | flops 4194304 | bytes 6291456 | tf_op jit(solution)/shard_map/convert_element_type | solution.py:48
  140.7 1.2 collective-permute-start
  141.9 8.8 %copy.20 = bf16[512,8,8,128]{3,1,2,0:T(8,128)(2,1)} copy(bf16[512,8,8,128]{3,2,1,0:T(8,128)(2,1)} %bitcast.67) | data formatting | bytes 16777216
  150.7 11.3 %copy.7 = bf16[1024,4096]{1,0:T(8,128)(2,1)} copy(bf16[1024,4096]{0,1:T(8,128)(2,1)} %bitcast.66) | data formatting | bytes 16777216 | tf_op jit(solution)/shard_map/dot_general | solution.py:53
  162.0 1.9 copy.21
  163.8 2.9 %copy.6 = bf16[256,4096]{1,0:T(8,128)(2,1)} copy(bf16[256,4096]{0,1:T(8,128)(2,1)S(1)} %bitcast.69) | data formatting | bytes 4194304 | tf_op jit(solution)/shard_map/dot_general | solution.py:54
  166.8 0.0 copy-start.1
  166.8 0.3 multiply_cosine_fusion
  167.2 25.0 %collective-permute-done = bf16[256,4096]{1,0:T(8,128)(2,1)} collective-permute-done((bf16[256,4096]{1,0:T(8,128)(2,1)}, bf16[256,4096]{1,0:T(8,128)(2,1)}, u32[]{:S(2)}, u32[]{:S(2)}) %collective-permute-start) | collective-permute-done | bytes 2097184 | tf_op jit(solution)/shard_map/ppermute | solution.py:15
  192.2 0.0 copy-start
  192.2 2.2 %fusion = f32[256]{0:T(256)S(1)} fusion(bf16[256,4096]{1,0:T(8,128)(2,1)} %collective-permute-done), kind=kLoop, calls=%fused_computation.3 | loop fusion | flops 3145472 | bytes 2098176 | tf_op jit(solution)/shard_map/reduce_sum | solution.py:51
  194.4 0.0 copy-done.1
  194.4 3.6 %convolution_bitcast_fusion.1 = f32[256,1,2,128]{0,3,2,1:T(8,128)S(1)} fusion(bf16[2,128,4096]{2,1,0:T(8,128)(2,1)} %bitcast.72, bf16[256,4096]{1,0:T(8,128)(2,1)} %collective-permute-done, f32[4096]{0:T(1024)S(1)} %bitcast.73, f32[256]{0:T(256)S(1)} %add_rsqrt_fusion), kind=kOutput, calls=%fused_computation.17 | convolution fusion | flops 541065216 | bytes 4473856 | tf_op jit(solution)/shard_map/dot_general | solution.py:54
  198.0 0.3 fusion.28
  198.4 0.0 copy-done
  198.4 4.0 %convolution_bitcast_fusion = f32[256,1,8,128]{0,3,2,1:T(8,128)S(1)} fusion(bf16[8,128,4096]{2,1,0:T(8,128)(2,1)S(1)} %bitcast.68, bf16[256,4096]{1,0:T(8,128)(2,1)} %collective-permute-done, f32[4096]{0:T(1024)S(1)} %bitcast.74, f32[256]{0:T(256)S(1)} %add_rsqrt_fusion), kind=kOutput, calls=%fused_computation.14 | convolution fusion | flops 2151677952 | bytes 11551744 | tf_op jit(solution)/shard_map/dot_general | solution.py:53
  202.4 0.1 fusion.13
  202.6 0.5 fusion.30
  203.0 0.3 fusion.5
  203.3 0.5 fusion.6
  203.9 1.1 copy.11
  (5 shorter events, 0.1 us)
Async XLA Ops:
  6.5 90.6 %all-reduce.2.cloned.1.call-start = ((), (), s32[]{:S(2)}) async-start(), calls=%async_computation | async-start | bytes 4194304 | tf_op jit(solution)/shard_map/psum | solution.py:46
  7.3 129.1 %all-gather.3.cloned.1.call-start = ((), (), s32[]{:S(2)}) async-start(), calls=%async_computation.1 | async-start | bytes 2359296 | tf_op jit(solution)/shard_map/all_gather | solution.py:47
  140.7 51.5 %collective-permute-start = (bf16[256,4096]{1,0:T(8,128)(2,1)}, bf16[256,4096]{1,0:T(8,128)(2,1)}, u32[]{:S(2)}, u32[]{:S(2)}) collective-permute-start(bf16[256,4096]{1,0:T(8,128)(2,1)} %fusion.3), channel_id=1, source_target_pairs={{0,8},{8,16},{16,24},{24,32},{32,40},{40,48},{48,56},{56,64},{64,7... | collective-permute-start | bytes 6291464 | tf_op jit(solution)/shard_map/ppermute | solution.py:15
  166.8 27.7 %copy-start.1 = (f32[1,4096]{1,0:T(1,128)S(1)}, f32[1,4096]{1,0:T(1,128)}, u32[]{:S(2)}) copy-start(f32[1,4096]{1,0:T(1,128)} %param.7) | copy-start | bytes 49156
  192.2 6.2 %copy-start = (bf16[1024,4096]{1,0:T(8,128)(2,1)S(1)}, bf16[1024,4096]{1,0:T(8,128)(2,1)}, u32[]{:S(2)}) copy-start(bf16[1024,4096]{1,0:T(8,128)(2,1)} %copy.7) | copy-start | bytes 25165828
Sparse Core Ops, SparseCore 0:
  10.0 87.1 all-reduce.1
  99.0 37.2 all-gather.2
where the time goes:
time: 212 us
  waiting for transfers between devices  155 us (73%)
  local copies, waits for them, and re-layouts  26 us (12%)
  between operations  13.5 us (6%)
  matrix products  8.6 us (4%)
  other arithmetic  7.69 us (4%)
    psum x1, waiting for transfers between devices, per_device(): summed = lax.psum(local_term.astype(jnp.bfloat16), 'tp').astype(jnp.float32)  89.2 us
    all_gather x1, waiting for transfers between devices, per_device(): residual_full = lax.all_gather(residual[0], 'tp', axis=0, tiled=True)  39.2 us
    ppermute x1, waiting for transfers between devices, from_behind(): return lax.ppermute(value, axis, pairs)  25 us
    dot_general x1, local copies, waits for them, and re-layouts, per_device(): queries = jnp.dot(normed, query_matrix, preferred_element_type=jnp.float32)  11.3 us
    unnamed x6, local copies, waits for them, and re-layouts  10.6 us
    convert_element_type x1, other arithmetic, per_device(): made = (summed + residual_full.astype(jnp.float32)).astype(jnp.bfloat16)  4.35 us
  transfers between devices with their start and end apart: 3, of which 3 were waited for; matrix products, arithmetic and copies ran while one was open for 12% of the time, Pallas kernels for 0%

commit v1 on v0

v1 whole, which is shorter than its diff:
```python
import functools
import math

import jax
import jax.numpy as jnp
from jax import lax
from jax.experimental import pallas as pl
from jax.experimental.pallas import tpu as pltpu
from jax.sharding import PartitionSpec as P

ROPE_BASE = 500000.0
NORM_EPS = 1e-05
CHIPS = 4
CORES = 2


def hop(value, chips, flip):
    pairs = []
    for rank in range(CHIPS * CORES):
        chip, core = divmod(rank, CORES)
        pairs.append((rank, (chip + chips) % CHIPS * CORES + (core ^ flip)))
    return lax.ppermute(value, "tp", pairs)


def next_section(value):
    count = lax.axis_size("segment")
    return lax.ppermute(value, "segment", [(s, (s + 1) % count) for s in range(count)])


def add(*terms):
    return sum(term.astype(jnp.float32) for term in terms).astype(jnp.bfloat16)


def rope(x, cosine, sine):
    half = x.shape[-1] // 2
    return x * cosine + pltpu.roll(x, half, 1) * sine


def attend_kernel(place_ref, own0, own1, own3, own2a, own2b, oth0, oth1, oth3, oth2a, oth2b,
                  cos_ref, sin_ref, wkv_ref, wq_ref, out_ref, rows, keys, values, heads):
    step = pl.program_id(0)
    head_dim = keys.shape[1]

    @pl.when(step == 0)
    def _():
        chip, core = place_ref[0], place_ref[1]
        for mine, (p0, p1, p3, p2a, p2b) in (
            (core, (own0, own1, own3, own2a, own2b)),
            (1 - core, (oth0, oth1, oth3, oth2a, oth2b)),
        ):
            for ahead, low, piece in ((0, 0, p0), (1, 0, p1), (3, 0, p3), (2, 0, p2a), (2, 16, p2b)):
                start = lax.rem(chip + ahead, CHIPS) * 64 + mine * 32 + low
                rows[pl.ds(pl.multiple_of(start, 16), piece.shape[0]), :] = piece[...]
        kv = jnp.dot(rows[...], wkv_ref[...], preferred_element_type=jnp.float32)
        keys[...] = rope(kv[:, :head_dim], cos_ref[...], sin_ref[...]).astype(jnp.bfloat16)
        values[...] = kv[:, head_dim:].astype(jnp.bfloat16)

    q = jnp.dot(rows[...], wq_ref[...], preferred_element_type=jnp.float32)
    tokens = q.shape[0]
    causal = lax.broadcasted_iota(jnp.int32, (tokens, tokens), 0) >= lax.broadcasted_iota(
        jnp.int32, (tokens, tokens), 1
    )
    per_step = q.shape[1] // head_dim
    for h in range(per_step):
        qh = rope(q[:, h * head_dim:(h + 1) * head_dim], cos_ref[...], sin_ref[...]).astype(jnp.bfloat16)
        scores = lax.dot_general(
            qh, keys[...], (((1,), (1,)), ((), ())), preferred_element_type=jnp.float32
        ) * (1.0 / math.sqrt(head_dim))
        scores = jnp.where(causal, scores, -jnp.inf)
        weights = jnp.exp(scores - jnp.max(scores, axis=-1, keepdims=True))
        probs = (weights / jnp.sum(weights, axis=-1, keepdims=True)).astype(jnp.bfloat16)
        heads[step * per_step + h] = jnp.dot(probs, values[...], preferred_element_type=jnp.float32)

    @pl.when(step == pl.num_programs(0) - 1)
    def _():
        for h in range(heads.shape[0]):
            out_ref[:, h, :] = heads[h].astype(jnp.bfloat16)


def per_device(partials, residual, norm_gain, w_query, w_keyval):
    tokens, width = partials.shape[2:]
    group, head_dim = w_query.shape[3:]
    rank = lax.axis_index("tp")
    chip, core = rank // CORES, rank % CORES
    blocks = partials[0, 0].reshape(CHIPS, CORES, tokens // (CHIPS * CORES), width)

    def block(ahead, which):
        return lax.dynamic_slice(
            blocks, (lax.rem(chip + ahead, CHIPS), which, 0, 0), (1, 1) + blocks.shape[2:]
        )[0, 0]

    far = add(block(2, core), hop(block(2, 1 - core), 0, 1))
    rest = hop(jnp.stack([block(d, 1 - core) for d in (1, 3, 0)]), 0, 1)
    up, down, here = (add(block(d, core), rest[i]) for i, d in enumerate((1, 3, 0)))
    low, high = hop(far[:16], 1, 0), hop(far[16:], -1, 0)
    from_below = hop(jnp.concatenate([add(up[:16], low), up[16:]]), 1, 0)
    from_above = hop(jnp.concatenate([down[:16], add(down[16:], high)]), -1, 0)
    made = add(here, from_below, from_above, residual[0])
    stream = next_section(made).astype(jnp.float32)
    mean_sq = jnp.mean(stream * stream, axis=-1, keepdims=True)
    own0 = (stream * lax.rsqrt(mean_sq + NORM_EPS) * norm_gain).astype(jnp.bfloat16)
    oth0 = hop(own0, 0, 1)
    own3, own1 = hop(own0, 1, 0), hop(own0, -1, 0)
    oth3, oth1 = hop(own3, 0, 1), hop(own1, 0, 1)
    own2a, own2b = hop(own3[:16], 1, 0), hop(own1[16:], -1, 0)
    oth2a, oth2b = hop(own2a, 0, 1), hop(own2b, 0, 1)

    half = head_dim // 2
    frequency = ROPE_BASE ** (-jnp.arange(half, dtype=jnp.float32) * 2.0 / head_dim)
    angles = jnp.arange(tokens).astype(jnp.float32)[:, None] * frequency[None, :]
    cosine = jnp.concatenate([jnp.cos(angles)] * 2, axis=1)
    sine = jnp.concatenate([-jnp.sin(angles), jnp.sin(angles)], axis=1)
    wq = w_query.reshape(width, group * head_dim)
    wkv = w_keyval.reshape(width, 2 * head_dim)
    place = jnp.stack([chip, core]).astype(jnp.int32)

    steps = group // 2
    whole = lambda shape: pl.BlockSpec(shape, lambda j, *_: (0,) * len(shape))
    pieces = (own0, own1, own3, own2a, own2b, oth0, oth1, oth3, oth2a, oth2b)
    attended = pl.pallas_call(
        attend_kernel,
        grid_spec=pltpu.PrefetchScalarGridSpec(
            num_scalar_prefetch=1,
            grid=(steps,),
            in_specs=[whole(p.shape) for p in pieces]
            + [whole(cosine.shape), whole(sine.shape), whole(wkv.shape),
               pl.BlockSpec((width, 2 * head_dim), lambda j, *_: (0, j))],
            out_specs=whole((tokens, group, head_dim)),
            scratch_shapes=[
                pltpu.VMEM((tokens, width), jnp.bfloat16),
                pltpu.VMEM((tokens, head_dim), jnp.bfloat16),
                pltpu.VMEM((tokens, head_dim), jnp.bfloat16),
                pltpu.VMEM((group, tokens, head_dim), jnp.float32),
            ],
        ),
        out_shape=jax.ShapeDtypeStruct((tokens, group, head_dim), jnp.bfloat16),
        compiler_params=pltpu.CompilerParams(vmem_limit_bytes=32 * 2**20),
        cost_estimate=pl.CostEstimate(
            flops=2 * tokens * width * (group + 2) * head_dim, bytes_accessed=14 * 2**20, transcendentals=0
        ),
    )(place, *pieces, cosine, sine, wkv, wq)
    return attended.reshape(1, tokens, 1, group, head_dim)


def solution(mesh):
    placed = (
        P("segment", "tp", None, None),
        P("segment", "tp", None),
        P("segment", None),
        P("segment", None, "tp", None, None),
        P("segment", None, "tp", None, None),
    )
    return jax.shard_map(
        per_device,
        mesh=mesh,
        in_specs=placed,
        out_specs=P("segment", None, "tp", None, None),
        check_vma=False,
    )
```

time: 212 us -> 99.6 us (0.47)
  waiting for transfers between devices: 155 us -> 36.9 us
  starting transfers between devices: 1.25 us -> 31.3 us
  between operations: 13.5 us -> 0.21 us
  Pallas kernels: 0 us -> 12.8 us
  local copies, waits for them, and re-layouts: 26 us -> 13.9 us
  matrix products: 8.6 us -> 0 us
  other arithmetic: 7.69 us -> 3.59 us
    psum x1 -> x0, waiting for transfers between devices: 89.2 us -> none  [per_device(): summed = lax.psum(local_term.astype(jnp.bfloat16), 'tp').astype(jnp.float32)]
    all_gather x1 -> x0, waiting for transfers between devices: 39.2 us -> none  [per_device(): residual_full = lax.all_gather(residual[0], 'tp', axis=0, tiled=True)]
    ppermute x1 -> x16, starting transfers between devices: 1.21 us -> 31.3 us  [the longest x15 23.9 us: hop(): return lax.ppermute(value, 'tp', pairs)]
    dot_general x2 -> x0, local copies, waits for them, and re-layouts: 14.2 us -> none  [the longest x1 11.3 us: per_device(): queries = jnp.dot(normed, query_matrix, preferred_element_type=jnp.float32)]
    pallas_call x0 -> x1, Pallas kernels: none -> 12.8 us  [per_device(): pl.pallas_call(attend_kernel, grid_spec=pltpu.PrefetchScalarGridSpec(num_...]
    ppermute x1 -> x16, waiting for transfers between devices: 25 us -> 36.9 us  [the longest x15 28.5 us: hop(): return lax.ppermute(value, 'tp', pairs)]
    dot_general x4 -> x0, matrix products: 8.6 us -> none  [the longest x1 4.03 us: per_device(): queries = jnp.dot(normed, query_matrix, preferred_element_type=jnp.float32)]
    reduce_sum x2 -> x1, other arithmetic: 2.53 us -> 0.17 us  [per_device(): mean_sq = jnp.mean(stream * stream, axis=-1, keepdims=True)]
  transfers between devices with their start and end apart: 3 -> 16, of which waited for: 3 -> 6; matrix products, arithmetic and copies ran while one was open for 12% -> 10% of each run, Pallas kernels for 0% -> 0%
where the time goes in v1:
time: 99.6 us; the launch traced here: 98.8 us
  waiting for transfers between devices  36.9 us (37%)
  starting transfers between devices  31.3 us (31%)
  local copies, waits for them, and re-layouts  13.9 us (14%)
  Pallas kernels  12.8 us (13%)
  other arithmetic  3.59 us (4%)
    ppermute x15, waiting for transfers between devices, hop(): return lax.ppermute(value, 'tp', pairs)  28.5 us
    ppermute x15, starting transfers between devices, hop(): return lax.ppermute(value, 'tp', pairs)  23.9 us
    pallas_call x1, Pallas kernels, per_device(): pl.pallas_call(attend_kernel, grid_spec=pltpu.PrefetchScalarGridSpec(num_...  12.8 us
    unnamed x12, local copies, waits for them, and re-layouts  12.5 us
    ppermute x1, waiting for transfers between devices, next_section(): lax.ppermute(value, 'segment', [(s, (s + 1) % count) for s in range(count)])  8.41 us
    ppermute x1, starting transfers between devices, next_section(): lax.ppermute(value, 'segment', [(s, (s + 1) % count) for s in range(count)])  7.46 us
    convert_element_type x4, other arithmetic, add(): sum((term.astype(jnp.float32) for term in terms)).astype(jnp.bfloat16)  2.4 us
  transfers between devices with their start and end apart: 16, of which 6 were waited for; matrix products, arithmetic and copies ran while one was open for 10% of the time, Pallas kernels for 0%

profile of v1, /device:TPU:1, one launch (start us, length us, event | category | flops | bytes accessed | tf_op | source)
XLA Modules:
  0.0 98.8 jit_solution(18150313059994396198)
XLA Ops:
  0.0 1.4 %dynamic-slice_bitcast_fusion.3 = (bf16[1,32,4096]{2,1,0:T(8,128)(2,1)S(1)}, bf16[32,4096]{1,0:T(8,128)(2,1)S(1)}, bf16[1,32,4096]{2,1,0:T(8,128)(2,1)S(1)}, bf16[1,32,4096]{2,1,0:T(8,128)(2,1)S(1)}) fusion(bf16[4,2,32,4096]{3,2,1,0:T(8,128)(2,1)} %bitcast.58, s32[]{:T(128)S(6)} %select_n.43, s32[]{:T(128)S(6)} %select_n.44, s32[]{:T(128)S(6)} %select_n.46, ...), kind=kLoop, calls=%fused_computation.28 | loop fusion | bytes 2097172 | tf_op jit(solution)/shard_map/stack;squeeze | solution.py:93
  1.4 0.1 pad_maximum_fusion
  1.5 3.3 %collective-permute-start = (bf16[3,32,4096]{2,1,0:T(8,128)(2,1)S(1)}, bf16[3,32,4096]{2,1,0:T(8,128)(2,1)}, u32[]{:S(2)}, u32[]{:S(2)}) collective-permute-start(bf16[3,32,4096]{2,1,0:T(8,128)(2,1)S(1)} %pad_maximum_fusion), channel_id=1, source_target_pairs={{0,1},{1,0},{2,3},{3,2},{4,5},{5,4},{6,7},{7,6},{8,9},{9,8},{10,11... | collective-permute-start | bytes 2359304 | tf_op jit(solution)/shard_map/ppermute | solution.py:22
  4.9 0.1 collective-permute-start.1
  5.0 2.2 %collective-permute-done.1 = bf16[32,4096]{1,0:T(8,128)(2,1)S(1)} collective-permute-done((bf16[32,4096]{1,0:T(8,128)(2,1)S(1)}, bf16[32,4096]{1,0:T(8,128)(2,1)S(1)}, u32[]{:S(2)}, u32[]{:S(2)}) %collective-permute-start.1) | collective-permute-done | bytes 262176 | tf_op jit(solution)/shard_map/ppermute | solution.py:22
  7.1 0.0 collective-permute-done
  7.1 0.0 copy-done.1
  7.1 1.2 %fusion.6 = (bf16[32,4096]{1,0:T(8,128)(2,1)S(1)}, bf16[32,4096]{1,0:T(8,128)(2,1)S(1)}, bf16[32,4096]{1,0:T(8,128)(2,1)S(1)}) fusion(bf16[3,32,4096]{2,1,0:T(8,128)(2,1)} %collective-permute-done, bf16[4,2,32,4096]{3,2,1,0:T(8,128)(2,1)S(1)} %bitcast.59, s32[]{:T(128)S(6)} %select_n.43, s32[]{:T(128)S(6)} %select_n.42, s32[]{:T(128)S(6)} %select_n.45, ...), kind=kLoop, calls=%fused_computation.15 | loop fusion | flops 1572864 | bytes 2359312 | tf_op jit(solution)/shard_map/convert_element_type | solution.py:31
  8.4 4.4 %collective-permute-start.4 = (bf16[16,4096]{1,0:T(8,128)(2,1)S(1)}, bf16[16,4096]{1,0:T(8,128)(2,1)S(1)}, u32[]{:S(2)}, u32[]{:S(2)}) collective-permute-start(bf16[16,4096]{1,0:T(8,128)(2,1)S(1)} %get-tuple-element.13), channel_id=1, source_target_pairs={{0,6},{1,7},{2,0},{3,1},{4,2},{5,3},{6,4},{7,5},{8,14},{9,15},{10,... | collective-permute-start | bytes 393224 | tf_op jit(solution)/shard_map/ppermute | solution.py:22
  12.8 0.1 collective-permute-start.2
  12.9 4.5 %collective-permute-done.4 = bf16[16,4096]{1,0:T(8,128)(2,1)S(1)} collective-permute-done((bf16[16,4096]{1,0:T(8,128)(2,1)S(1)}, bf16[16,4096]{1,0:T(8,128)(2,1)S(1)}, u32[]{:S(2)}, u32[]{:S(2)}) %collective-permute-start.4) | collective-permute-done | bytes 131104 | tf_op jit(solution)/shard_map/ppermute | solution.py:22
  17.4 0.0 copy-start.2
  17.4 3.1 %collective-permute-start.5 = (bf16[32,4096]{1,0:T(8,128)(2,1)S(1)}, bf16[32,4096]{1,0:T(8,128)(2,1)S(1)}, u32[]{:S(2)}, u32[]{:S(2)}) collective-permute-start(bf16[32,4096]{1,0:T(8,128)(2,1)S(1)} %pad_maximum_fusion.2), channel_id=1, source_target_pairs={{0,6},{1,7},{2,0},{3,1},{4,2},{5,3},{6,4},{7,5},{8,14},{9,15},{10,... | collective-permute-start | bytes 786440 | tf_op jit(solution)/shard_map/ppermute | solution.py:22
  20.5 0.0 collective-permute-done.2
  20.6 0.1 collective-permute-start.3
  20.7 10.8 %collective-permute-done.5 = bf16[32,4096]{1,0:T(8,128)(2,1)S(1)} collective-permute-done((bf16[32,4096]{1,0:T(8,128)(2,1)S(1)}, bf16[32,4096]{1,0:T(8,128)(2,1)S(1)}, u32[]{:S(2)}, u32[]{:S(2)}) %collective-permute-start.5) | collective-permute-done | bytes 262176 | tf_op jit(solution)/shard_map/ppermute | solution.py:22
  31.4 0.0 collective-permute-done.3
  31.5 1.1 %fusion.3 = bf16[32,4096]{1,0:T(8,128)(2,1)S(1)} fusion(bf16[32,4096]{1,0:T(8,128)(2,1)S(1)} %collective-permute-done.5, bf16[32,4096]{1,0:T(8,128)(2,1)S(1)} %collective-permute-done.3, bf16[3,32,4096]{2,1,0:T(8,128)(2,1)} %collective-permute-done, bf16[1,32,4096]{2,1,0:T(8,128)(2,1)S(1)} %copy-done.3, bf16[4,2,32,4096]{3,2,1,0:T(8,128)(2,1)S(1)} %bitcast.60, ...), kind=kLoop, calls=%fused_computation.9 | loop fusion | flops 1572864 | bytes 1572872 | tf_op jit(solution)/shard_map/convert_element_type | solution.py:31
  32.6 7.5 %collective-permute-start.6 = (bf16[32,4096]{1,0:T(8,128)(2,1)S(1)}, bf16[32,4096]{1,0:T(8,128)(2,1)S(1)}, u32[]{:S(2)}, u32[]{:S(2)}) collective-permute-start(bf16[32,4096]{1,0:T(8,128)(2,1)S(1)} %fusion.3), channel_id=1, source_target_pairs={{0,8},{8,16},{16,24},{24,32},{32,40},{40,48},{48,56},{56,64},{64,7... | collective-permute-start | bytes 786440 | tf_op jit(solution)/shard_map/ppermute | solution.py:27
  40.0 8.4 %collective-permute-done.6 = bf16[32,4096]{1,0:T(8,128)(2,1)S(1)} collective-permute-done((bf16[32,4096]{1,0:T(8,128)(2,1)S(1)}, bf16[32,4096]{1,0:T(8,128)(2,1)S(1)}, u32[]{:S(2)}, u32[]{:S(2)}) %collective-permute-start.6) | collective-permute-done | bytes 262176 | tf_op jit(solution)/shard_map/ppermute | solution.py:27
  48.5 0.2 fusion
  48.6 0.0 copy-done.4
  48.6 0.1 fusion.2.own0
  48.8 0.6 collective-permute-start.8
  49.3 3.1 %collective-permute-start.7 = (bf16[32,4096]{1,0:T(8,128)(2,1)S(1)}, bf16[32,4096]{1,0:T(8,128)(2,1)S(1)}, u32[]{:S(2)}, u32[]{:S(2)}) collective-permute-start(bf16[32,4096]{1,0:T(8,128)(2,1)S(1)} %fusion.2.own0), channel_id=1, source_target_pairs={{0,6},{1,7},{2,0},{3,1},{4,2},{5,3},{6,4},{7,5},{8,14},{9,15},{10,... | collective-permute-start | bytes 786440 | tf_op jit(solution)/shard_map/ppermute | solution.py:22
  52.4 2.6 %collective-permute-start.11 = (bf16[32,4096]{1,0:T(8,128)(2,1)S(1)}, bf16[32,4096]{1,0:T(8,128)(2,1)S(1)}, u32[]{:S(2)}, u32[]{:S(2)}) collective-permute-start(bf16[32,4096]{1,0:T(8,128)(2,1)S(1)} %fusion.2.own0), channel_id=1, source_target_pairs={{0,1},{1,0},{2,3},{3,2},{4,5},{5,4},{6,7},{7,6},{8,9},{9,8},{10,11... | collective-permute-start | bytes 786440 | tf_op jit(solution)/shard_map/ppermute | solution.py:22
  55.0 9.7 %collective-permute-done.8.own3 = bf16[32,4096]{1,0:T(8,128)(2,1)S(1)} collective-permute-done((bf16[32,4096]{1,0:T(8,128)(2,1)S(1)}, bf16[32,4096]{1,0:T(8,128)(2,1)S(1)}, u32[]{:S(2)}, u32[]{:S(2)}) %collective-permute-start.8) | collective-permute-done | bytes 262176 | tf_op jit(solution)/shard_map/ppermute | solution.py:22
  64.8 0.1 collective-permute-start.9
  64.9 0.0 collective-permute-done.7.own1
  64.9 3.6 %collective-permute-start.10 = (bf16[16,4096]{1,0:T(8,128)(2,1)S(1)}, bf16[16,4096]{1,0:T(8,128)(2,1)S(1)}, u32[]{:S(2)}, u32[]{:S(2)}) collective-permute-start(bf16[16,4096]{1,0:T(8,128)(2,1)S(1)} %slice.54), channel_id=1, source_target_pairs={{0,6},{1,7},{2,0},{3,1},{4,2},{5,3},{6,4},{7,5},{8,14},{9,15},{10,... | collective-permute-start | bytes 393224 | tf_op jit(solution)/shard_map/ppermute | solution.py:22
  68.5 1.1 %collective-permute-start.13 = (bf16[32,4096]{1,0:T(8,128)(2,1)S(1)}, bf16[32,4096]{1,0:T(8,128)(2,1)S(1)}, u32[]{:S(2)}, u32[]{:S(2)}) collective-permute-start(bf16[32,4096]{1,0:T(8,128)(2,1)S(1)} %collective-permute-done.8.own3), channel_id=1, source_target_pairs={{0,1},{1,0},{2,3},{3,2},{4,5},{5,4},{6,7},{7,6},{8,9},{9,8},{10,11... | collective-permute-start | bytes 786440 | tf_op jit(solution)/shard_map/ppermute | solution.py:22
  69.6 0.0 collective-permute-start.12
  69.6 0.5 fusion.8
  70.2 1.3 %collective-permute-done.9.own2a = bf16[16,4096]{1,0:T(8,128)(2,1)S(1)} collective-permute-done((bf16[16,4096]{1,0:T(8,128)(2,1)S(1)}, bf16[16,4096]{1,0:T(8,128)(2,1)S(1)}, u32[]{:S(2)}, u32[]{:S(2)}) %collective-permute-start.9) | collective-permute-done | bytes 131104 | tf_op jit(solution)/shard_map/ppermute | solution.py:22
  71.5 1.4 %collective-permute-start.14 = (bf16[16,4096]{1,0:T(8,128)(2,1)S(1)}, bf16[16,4096]{1,0:T(8,128)(2,1)S(1)}, u32[]{:S(2)}, u32[]{:S(2)}) collective-permute-start(bf16[16,4096]{1,0:T(8,128)(2,1)S(1)} %collective-permute-done.9.own2a), channel_id=1, source_target_pairs={{0,1},{1,0},{2,3},{3,2},{4,5},{5,4},{6,7},{7,6},{8,9},{9,8},{10,11... | collective-permute-start | bytes 393224 | tf_op jit(solution)/shard_map/ppermute | solution.py:22
  72.9 0.0 collective-permute-done.10.own2b
  72.9 0.4 collective-permute-start.15
  73.3 0.1 pad_add_fusion.place_ref
  73.4 0.3 copy.12
  73.7 8.8 %copy.11 = bf16[512,8,8,128]{3,1,2,0:T(8,128)(2,1)} copy(bf16[512,8,8,128]{3,2,1,0:T(8,128)(2,1)} %bitcast.57) | data formatting | bytes 16777216
  82.5 0.1 pad_maximum_fusion.3
  82.6 0.0 collective-permute-done.11.oth0
  82.6 0.0 collective-permute-done.13.oth3
  82.6 0.0 collective-permute-done.12.oth1
  82.6 0.0 collective-permute-done.14.oth2a
  82.6 0.0 collective-permute-done.15.oth2b
  82.7 3.4 %copy-done = bf16[512,8,8,128]{3,1,2,0:T(8,128)(2,1)S(1)} copy-done((bf16[512,8,8,128]{3,1,2,0:T(8,128)(2,1)S(1)}, bf16[512,8,8,128]{3,1,2,0:T(8,128)(2,1)}, u32[]{:S(2)}) %copy-start) | copy-done | bytes 8388632
  86.0 12.8 %shard_map.55 = bf16[256,8,128]{2,1,0:T(8,128)(2,1)} custom-call(s32[2]{0:T(128)S(1)} %pad_add_fusion.place_ref, bf16[32,4096]{1,0:T(8,128)(2,1)S(1)} %fusion.2.own0, bf16[32,4096]{1,0:T(8,128)(2,1)S(1)} %collective-permute-done.7.own1, bf16[32,4096]{1,0:T(8,128)(2,1)S(1)} %collective-permute-done.8.own3, bf16[16,4096]{1,0:T(8,128)(2,1)S(1)} %collective-permute-done.9.own2a, ...), custom_call_target="tpu_custom_call" | custom-call | flops 2684354560 | bytes 14680064 | tf_op jit(solution)/shard_map/pallas_call | solution.py:120
  (18 shorter events, 0.2 us)
Async XLA Ops:
  0.0 7.1 %copy-start.1 = (bf16[1,1,256,4096]{3,2,1,0:T(8,128)(2,1)S(1)}, bf16[1,1,256,4096]{3,2,1,0:T(8,128)(2,1)}, u32[]{:S(2)}) copy-start(bf16[1,1,256,4096]{3,2,1,0:T(8,128)(2,1)} %param.5) | copy-start | bytes 6291460
  1.5 5.6 %collective-permute-start = (bf16[3,32,4096]{2,1,0:T(8,128)(2,1)S(1)}, bf16[3,32,4096]{2,1,0:T(8,128)(2,1)}, u32[]{:S(2)}, u32[]{:S(2)}) collective-permute-start(bf16[3,32,4096]{2,1,0:T(8,128)(2,1)S(1)} %pad_maximum_fusion), channel_id=1, source_target_pairs={{0,1},{1,0},{2,3},{3,2},{4,5},{5,4},{6,7},{7,6},{8,9},{9,8},{10,11... | collective-permute-start | bytes 2359304 | tf_op jit(solution)/shard_map/ppermute | solution.py:22
  4.9 2.3 %collective-permute-start.1 = (bf16[32,4096]{1,0:T(8,128)(2,1)S(1)}, bf16[32,4096]{1,0:T(8,128)(2,1)S(1)}, u32[]{:S(2)}, u32[]{:S(2)}) collective-permute-start(bf16[32,4096]{1,0:T(8,128)(2,1)S(1)} %get-tuple-element.9), channel_id=1, source_target_pairs={{0,1},{1,0},{2,3},{3,2},{4,5},{5,4},{6,7},{7,6},{8,9},{9,8},{10,11... | collective-permute-start | bytes 786440 | tf_op jit(solution)/shard_map/ppermute | solution.py:22
  5.0 26.5 %copy-start.3 = (bf16[1,32,4096]{2,1,0:T(8,128)(2,1)S(1)}, bf16[1,32,4096]{2,1,0:T(8,128)(2,1)}, u32[]{:S(2)}) copy-start(bf16[1,32,4096]{2,1,0:T(8,128)(2,1)} %param.6) | copy-start | bytes 786436
  8.4 9.0 %collective-permute-start.4 = (bf16[16,4096]{1,0:T(8,128)(2,1)S(1)}, bf16[16,4096]{1,0:T(8,128)(2,1)S(1)}, u32[]{:S(2)}, u32[]{:S(2)}) collective-permute-start(bf16[16,4096]{1,0:T(8,128)(2,1)S(1)} %get-tuple-element.13), channel_id=1, source_target_pairs={{0,6},{1,7},{2,0},{3,1},{4,2},{5,3},{6,4},{7,5},{8,14},{9,15},{10,... | collective-permute-start | bytes 393224 | tf_op jit(solution)/shard_map/ppermute | solution.py:22
  12.8 35.9 %copy-start.4 = (f32[1,4096]{1,0:T(1,128)S(1)}, f32[1,4096]{1,0:T(1,128)}, u32[]{:S(2)}) copy-start(f32[1,4096]{1,0:T(1,128)} %param.7) | copy-start | bytes 49156
  12.8 7.7 %collective-permute-start.2 = (bf16[16,4096]{1,0:T(8,128)(2,1)S(1)}, bf16[16,4096]{1,0:T(8,128)(2,1)S(1)}, u32[]{:S(2)}, u32[]{:S(2)}) collective-permute-start(bf16[16,4096]{1,0:T(8,128)(2,1)S(1)} %get-tuple-element.12), channel_id=1, source_target_pairs={{0,2},{1,3},{2,4},{3,5},{4,6},{5,7},{6,0},{7,1},{8,10},{9,11},{10,... | collective-permute-start | bytes 393224 | tf_op jit(solution)/shard_map/ppermute | solution.py:22
  17.4 55.9 %copy-start.2 = (bf16[1,4096,1,2,128]{4,3,2,1,0:T(2,128)(2,1)S(1)}, bf16[1,4096,1,2,128]{4,3,2,1,0:T(2,128)(2,1)}, u32[]{:S(2)}) copy-start(bf16[1,4096,1,2,128]{4,3,2,1,0:T(2,128)(2,1)} %param.9) | copy-start | bytes 6291460
  17.4 14.0 %collective-permute-start.5 = (bf16[32,4096]{1,0:T(8,128)(2,1)S(1)}, bf16[32,4096]{1,0:T(8,128)(2,1)S(1)}, u32[]{:S(2)}, u32[]{:S(2)}) collective-permute-start(bf16[32,4096]{1,0:T(8,128)(2,1)S(1)} %pad_maximum_fusion.2), channel_id=1, source_target_pairs={{0,6},{1,7},{2,0},{3,1},{4,2},{5,3},{6,4},{7,5},{8,14},{9,15},{10,... | collective-permute-start | bytes 786440 | tf_op jit(solution)/shard_map/ppermute | solution.py:22
  20.6 10.9 %collective-permute-start.3 = (bf16[32,4096]{1,0:T(8,128)(2,1)S(1)}, bf16[32,4096]{1,0:T(8,128)(2,1)S(1)}, u32[]{:S(2)}, u32[]{:S(2)}) collective-permute-start(bf16[32,4096]{1,0:T(8,128)(2,1)S(1)} %pad_maximum_fusion.1), channel_id=1, source_target_pairs={{0,2},{1,3},{2,4},{3,5},{4,6},{5,7},{6,0},{7,1},{8,10},{9,11},{10,... | collective-permute-start | bytes 786440 | tf_op jit(solution)/shard_map/ppermute | solution.py:22
  32.6 15.9 %collective-permute-start.6 = (bf16[32,4096]{1,0:T(8,128)(2,1)S(1)}, bf16[32,4096]{1,0:T(8,128)(2,1)S(1)}, u32[]{:S(2)}, u32[]{:S(2)}) collective-permute-start(bf16[32,4096]{1,0:T(8,128)(2,1)S(1)} %fusion.3), channel_id=1, source_target_pairs={{0,8},{8,16},{16,24},{24,32},{32,40},{40,48},{48,56},{56,64},{64,7... | collective-permute-start | bytes 786440 | tf_op jit(solution)/shard_map/ppermute | solution.py:27
  48.8 16.0 %collective-permute-start.8 = (bf16[32,4096]{1,0:T(8,128)(2,1)S(1)}, bf16[32,4096]{1,0:T(8,128)(2,1)S(1)}, u32[]{:S(2)}, u32[]{:S(2)}) collective-permute-start(bf16[32,4096]{1,0:T(8,128)(2,1)S(1)} %fusion.2.own0), channel_id=1, source_target_pairs={{0,2},{1,3},{2,4},{3,5},{4,6},{5,7},{6,0},{7,1},{8,10},{9,11},{10,... | collective-permute-start | bytes 786440 | tf_op jit(solution)/shard_map/ppermute | solution.py:22
  49.3 15.5 %collective-permute-start.7 = (bf16[32,4096]{1,0:T(8,128)(2,1)S(1)}, bf16[32,4096]{1,0:T(8,128)(2,1)S(1)}, u32[]{:S(2)}, u32[]{:S(2)}) collective-permute-start(bf16[32,4096]{1,0:T(8,128)(2,1)S(1)} %fusion.2.own0), channel_id=1, source_target_pairs={{0,6},{1,7},{2,0},{3,1},{4,2},{5,3},{6,4},{7,5},{8,14},{9,15},{10,... | collective-permute-start | bytes 786440 | tf_op jit(solution)/shard_map/ppermute | solution.py:22
  52.4 30.2 %collective-permute-start.11 = (bf16[32,4096]{1,0:T(8,128)(2,1)S(1)}, bf16[32,4096]{1,0:T(8,128)(2,1)S(1)}, u32[]{:S(2)}, u32[]{:S(2)}) collective-permute-start(bf16[32,4096]{1,0:T(8,128)(2,1)S(1)} %fusion.2.own0), channel_id=1, source_target_pairs={{0,1},{1,0},{2,3},{3,2},{4,5},{5,4},{6,7},{7,6},{8,9},{9,8},{10,11... | collective-permute-start | bytes 786440 | tf_op jit(solution)/shard_map/ppermute | solution.py:22
  64.8 6.7 %collective-permute-start.9 = (bf16[16,4096]{1,0:T(8,128)(2,1)S(1)}, bf16[16,4096]{1,0:T(8,128)(2,1)S(1)}, u32[]{:S(2)}, u32[]{:S(2)}) collective-permute-start(bf16[16,4096]{1,0:T(8,128)(2,1)S(1)} %slice.53), channel_id=1, source_target_pairs={{0,2},{1,3},{2,4},{3,5},{4,6},{5,7},{6,0},{7,1},{8,10},{9,11},{10,... | collective-permute-start | bytes 393224 | tf_op jit(solution)/shard_map/ppermute | solution.py:22
  64.9 8.0 %collective-permute-start.10 = (bf16[16,4096]{1,0:T(8,128)(2,1)S(1)}, bf16[16,4096]{1,0:T(8,128)(2,1)S(1)}, u32[]{:S(2)}, u32[]{:S(2)}) collective-permute-start(bf16[16,4096]{1,0:T(8,128)(2,1)S(1)} %slice.54), channel_id=1, source_target_pairs={{0,6},{1,7},{2,0},{3,1},{4,2},{5,3},{6,4},{7,5},{8,14},{9,15},{10,... | collective-permute-start | bytes 393224 | tf_op jit(solution)/shard_map/ppermute | solution.py:22
  68.5 14.1 %collective-permute-start.13 = (bf16[32,4096]{1,0:T(8,128)(2,1)S(1)}, bf16[32,4096]{1,0:T(8,128)(2,1)S(1)}, u32[]{:S(2)}, u32[]{:S(2)}) collective-permute-start(bf16[32,4096]{1,0:T(8,128)(2,1)S(1)} %collective-permute-done.8.own3), channel_id=1, source_target_pairs={{0,1},{1,0},{2,3},{3,2},{4,5},{5,4},{6,7},{7,6},{8,9},{9,8},{10,11... | collective-permute-start | bytes 786440 | tf_op jit(solution)/shard_map/ppermute | solution.py:22
  69.6 13.0 %collective-permute-start.12 = (bf16[32,4096]{1,0:T(8,128)(2,1)S(1)}, bf16[32,4096]{1,0:T(8,128)(2,1)S(1)}, u32[]{:S(2)}, u32[]{:S(2)}) collective-permute-start(bf16[32,4096]{1,0:T(8,128)(2,1)S(1)} %collective-permute-done.7.own1), channel_id=1, source_target_pairs={{0,1},{1,0},{2,3},{3,2},{4,5},{5,4},{6,7},{7,6},{8,9},{9,8},{10,11... | collective-permute-start | bytes 786440 | tf_op jit(solution)/shard_map/ppermute | solution.py:22
  71.5 11.1 %collective-permute-start.14 = (bf16[16,4096]{1,0:T(8,128)(2,1)S(1)}, bf16[16,4096]{1,0:T(8,128)(2,1)S(1)}, u32[]{:S(2)}, u32[]{:S(2)}) collective-permute-start(bf16[16,4096]{1,0:T(8,128)(2,1)S(1)} %collective-permute-done.9.own2a), channel_id=1, source_target_pairs={{0,1},{1,0},{2,3},{3,2},{4,5},{5,4},{6,7},{7,6},{8,9},{9,8},{10,11... | collective-permute-start | bytes 393224 | tf_op jit(solution)/shard_map/ppermute | solution.py:22
  72.9 9.8 %collective-permute-start.15 = (bf16[16,4096]{1,0:T(8,128)(2,1)S(1)}, bf16[16,4096]{1,0:T(8,128)(2,1)S(1)}, u32[]{:S(2)}, u32[]{:S(2)}) collective-permute-start(bf16[16,4096]{1,0:T(8,128)(2,1)S(1)} %collective-permute-done.10.own2b), channel_id=1, source_target_pairs={{0,1},{1,0},{2,3},{3,2},{4,5},{5,4},{6,7},{7,6},{8,9},{9,8},{10,11... | collective-permute-start | bytes 393224 | tf_op jit(solution)/shard_map/ppermute | solution.py:22
  82.6 3.4 %copy-start = (bf16[512,8,8,128]{3,1,2,0:T(8,128)(2,1)S(1)}, bf16[512,8,8,128]{3,1,2,0:T(8,128)(2,1)}, u32[]{:S(2)}) copy-start(bf16[512,8,8,128]{3,1,2,0:T(8,128)(2,1)} %copy.11) | copy-start | bytes 25165828

commit v2 on v0

v2 whole, which is shorter than its diff:
```python
import functools
import math

import jax
import jax.numpy as jnp
from jax import lax
from jax.experimental import pallas as pl
from jax.experimental.pallas import tpu as pltpu
from jax.sharding import PartitionSpec as P

ROPE_BASE = 500000.0
NORM_EPS = 1e-05
CHIPS = 4
CORES = 2
FOLD = 16


def partner(step, chip, core):
    return chip ^ 1 if core == step else CHIPS - 1 - chip


def send(value, step=None, flip=0, sections=(0, 0), cores=(0, 1)):
    ranks = CHIPS * CORES
    count = lax.axis_size("segment")
    pairs = []
    for rank in range(ranks):
        chip, core = divmod(rank, CORES)
        chip = chip if step is None else partner(step, chip, core)
        if core in cores:
            pairs.append((rank, chip * CORES + (core ^ flip), sections[core]))
    if not any(sections):
        return lax.ppermute(value, "tp", [pair[:2] for pair in pairs])
    both = [(s * ranks + a, (s + ahead) % count * ranks + b) for s in range(count) for a, b, ahead in pairs]
    return lax.ppermute(value, ("segment", "tp"), both)


IN_VMEM = pl.BlockSpec(memory_space=pltpu.VMEM)
IN_SMEM = pl.BlockSpec(memory_space=pltpu.SMEM)
IN_HBM = pl.BlockSpec(memory_space=pltpu.HBM)
ANYWHERE = pl.BlockSpec(memory_space=pl.ANY)


def total(*terms):
    return sum(term.astype(jnp.float32) for term in terms)


def sum_kernel(count, *refs):
    refs[-1][...] = total(*(ref[...] for ref in refs[:count])).astype(refs[-1].dtype)


def sum_after(terms, *earlier):
    return pl.pallas_call(
        functools.partial(sum_kernel, len(terms)),
        in_specs=[IN_VMEM] * len(terms) + [ANYWHERE] * len(earlier),
        out_specs=IN_VMEM,
        out_shape=jax.ShapeDtypeStruct(terms[0].shape, jnp.bfloat16),
        compiler_params=pltpu.CompilerParams(vmem_limit_bytes=4 * 2**20),
    )(*terms, *earlier)


def rope(x, cosine, sine):
    return x * cosine + pltpu.roll(x, x.shape[-1] // 2, 1) * sine


def weights_kernel(wq_in, wkv_in, gain_ref, *refs):
    wq_out, wkv_out = refs[-2:]
    gain = gain_ref[...]
    for source, target in ((wq_in, wq_out), (wkv_in, wkv_out)):
        target[...] = (source[...].reshape(target.shape).astype(jnp.float32) * gain).astype(jnp.bfloat16)


def fold_weights(w_query, w_keyval, gain, *earlier):
    width, group, head_dim = w_query.shape
    depth = 512
    return pl.pallas_call(
        weights_kernel,
        grid=(width // depth,),
        in_specs=[
            pl.BlockSpec((depth, group, head_dim), lambda i: (i, 0, 0)),
            pl.BlockSpec((depth, 2, head_dim), lambda i: (i, 0, 0)),
            pl.BlockSpec((depth, 1), lambda i: (i, 0)),
        ]
        + [ANYWHERE] * len(earlier),
        out_specs=[
            pl.BlockSpec((depth, group * head_dim), lambda i: (i, 0)),
            pl.BlockSpec((depth, 2 * head_dim), lambda i: (i, 0)),
        ],
        out_shape=[
            pltpu.VMEM((width, group * head_dim), jnp.bfloat16),
            pltpu.VMEM((width, 2 * head_dim), jnp.bfloat16),
        ],
        compiler_params=pltpu.CompilerParams(vmem_limit_bytes=FOLD * 2**20),
        cost_estimate=pl.CostEstimate(flops=0, bytes_accessed=20 * 2**20, transcendentals=0),
    )(w_query, w_keyval, gain, *earlier)


def attend_kernel(place_ref, *refs):
    pieces, rest = refs[:8], refs[8:]
    cosq, sinq, cosk, sink, wkv_ref, wq_ref, out_ref, rows, queries, heads = rest
    tokens, width = rows.shape
    group, head_dim = out_ref.shape[1:]
    chip, core, one, two = place_ref[0], place_ref[1], place_ref[2], place_ref[3]
    per = pieces[0].shape[0]
    chips = (chip, chip, two, one, one, two, chip ^ 2, chip ^ 2)
    for index, (at, piece) in enumerate(zip(chips, pieces)):
        start = (at * CORES + (core ^ (index % CORES))) * per
        rows[pl.ds(pl.multiple_of(start, per), per), :] = piece[...]
    x = rows[...]
    squares = jnp.sum(jnp.square(x.astype(jnp.float32)), axis=-1, keepdims=True)
    scale = lax.rsqrt(squares * (1.0 / width) + NORM_EPS)
    kv = jnp.dot(x, wkv_ref[...], preferred_element_type=jnp.float32) * scale
    keys = rope(kv[:, :head_dim], cosk[...], sink[...]).astype(jnp.bfloat16)
    ones = jnp.ones((tokens, head_dim), jnp.bfloat16)
    values = jnp.concatenate([kv[:, head_dim:].astype(jnp.bfloat16), ones], axis=1)
    for pair in range(group // 2):
        cols = slice(pair * 2 * head_dim, (pair + 1) * 2 * head_dim)
        q = jnp.dot(x, wq_ref[:, cols], preferred_element_type=jnp.float32) * scale
        for h in range(2):
            turned = rope(q[:, h * head_dim:(h + 1) * head_dim], cosq[...], sinq[...])
            queries[pl.ds((2 * pair + h) * tokens, tokens), :] = turned.astype(jnp.bfloat16)
    causal = lax.broadcasted_iota(jnp.int32, (tokens, tokens), 0) >= lax.broadcasted_iota(
        jnp.int32, (tokens, tokens), 1
    )
    batch = 4
    causal = jnp.concatenate([causal] * batch, axis=0)
    for first in range(0, group, batch):
        scores = lax.dot_general(
            queries[pl.ds(first * tokens, batch * tokens), :], keys, (((1,), (1,)), ((), ())),
            preferred_element_type=jnp.float32,
        )
        scores = jnp.where(causal, scores, -jnp.inf)
        weights = jnp.exp2(scores - jnp.max(scores, axis=-1, keepdims=True)).astype(jnp.bfloat16)
        summed = jnp.dot(weights, values, preferred_element_type=jnp.float32)
        result = summed[:, :head_dim] / summed[:, head_dim:]
        for h in range(batch):
            heads[:, first + h, :] = result[h * tokens:(h + 1) * tokens]
    out_ref[...] = heads[...].astype(jnp.bfloat16)


def per_device(partials, residual, norm_gain, w_query, w_keyval):
    tokens, width = partials.shape[2:]
    group, head_dim = w_query.shape[3:]
    rank = lax.axis_index("tp")
    chip, core = rank >> 1, rank & 1
    blocks = partials[0, 0].reshape(CHIPS, CORES, tokens // (CHIPS * CORES), width)

    one = jnp.where(core == 0, chip ^ 1, CHIPS - 1 - chip)
    two = jnp.where(core == 0, CHIPS - 1 - chip, chip ^ 1)

    def block(at_chip, at_core):
        return lax.dynamic_slice(blocks, (at_chip, at_core, 0, 0), (1, 1) + blocks.shape[2:])[0, 0]

    place = jnp.stack([chip, core, one, two]).astype(jnp.int32)
    far_in = send(block(chip ^ 2, 1 - core), flip=1)
    one_in, two_in, here_in = (send(block(at, 1 - core), flip=1) for at in (two, one, chip))
    far_mine, one_mine, two_mine, here_mine = (block(at, core) for at in (chip ^ 2, one, two, chip))
    far_out = sum_after((far_mine, far_in))
    far = send(far_out, step=0)
    here = send(sum_after((here_mine, here_in, residual[0])), sections=(1, 1))
    near = send(sum_after((one_mine, one_in)), step=0, sections=(1, 1))
    last = send(sum_after((two_mine, two_in, far)), step=1, sections=(1, 1))
    made = sum_after((here, near, last))

    half = head_dim // 2
    frequency = ROPE_BASE ** (-jnp.arange(half, dtype=jnp.float32) * 2.0 / head_dim)
    angles = jnp.arange(tokens).astype(jnp.float32)[:, None] * frequency[None, :]
    cosine = jnp.concatenate([jnp.cos(angles)] * 2, axis=1)
    sine = jnp.concatenate([-jnp.sin(angles), jnp.sin(angles)], axis=1)
    fold = math.log2(math.e) / math.sqrt(head_dim)
    tables = (cosine * fold, sine * fold, cosine, sine)

    own2 = send(made, step=1)
    wq, wkv = fold_weights(w_query[0, :, 0], w_keyval[0, :, 0], norm_gain.reshape(width, 1), made)
    own1 = send(sum_after((made,), wq, wkv, *tables), step=0)
    own0 = made
    own3 = send(own2, step=0)
    pieces = []
    for piece in (own0, own2, own1, own3):
        pieces += [piece, send(piece, flip=1)]

    operands = (*pieces, *tables, wkv, wq)
    attended = pl.pallas_call(
        attend_kernel,
        in_specs=[IN_SMEM] + [IN_VMEM] * len(operands),
        out_specs=IN_VMEM,
        scratch_shapes=[
            pltpu.VMEM((tokens, width), jnp.bfloat16),
            pltpu.VMEM((group * tokens, head_dim), jnp.bfloat16),
            pltpu.VMEM((tokens, group, head_dim), jnp.float32),
        ],
        out_shape=jax.ShapeDtypeStruct((tokens, group, head_dim), jnp.bfloat16),
        compiler_params=pltpu.CompilerParams(vmem_limit_bytes=24 * 2**20),
        cost_estimate=pl.CostEstimate(
            flops=2 * tokens * width * (group + 2) * head_dim, bytes_accessed=14 * 2**20, transcendentals=0
        ),
    )(place, *operands)
    return attended.reshape(1, tokens, 1, group, head_dim)


def solution(mesh):
    placed = (
        P("segment", "tp", None, None),
        P("segment", "tp", None),
        P("segment", None),
        P("segment", None, "tp", None, None),
        P("segment", None, "tp", None, None),
    )
    return jax.shard_map(
        per_device,
        mesh=mesh,
        in_specs=placed,
        out_specs=P("segment", None, "tp", None, None),
        check_vma=False,
    )
```

time: 212 us -> 71.4 us (0.34)
  waiting for transfers between devices: 155 us -> 33 us
  starting transfers between devices: 1.25 us -> 21.6 us
  local copies, waits for them, and re-layouts: 26 us -> 5.71 us
  between operations: 13.5 us -> 0.13 us
  Pallas kernels: 0 us -> 9.99 us
  matrix products: 8.6 us -> 0 us
  other arithmetic: 7.69 us -> 0.76 us
    psum x1 -> x0, waiting for transfers between devices: 89.2 us -> none  [per_device(): summed = lax.psum(local_term.astype(jnp.bfloat16), 'tp').astype(jnp.float32)]
    all_gather x1 -> x0, waiting for transfers between devices: 39.2 us -> none  [per_device(): residual_full = lax.all_gather(residual[0], 'tp', axis=0, tiled=True)]
    ppermute x1 -> x15, starting transfers between devices: 1.21 us -> 21.6 us  [the longest x12 15.9 us: send(): return lax.ppermute(value, 'tp', [pair[:2] for pair in pairs])]
    dot_general x2 -> x0, local copies, waits for them, and re-layouts: 14.2 us -> none  [the longest x1 11.3 us: per_device(): queries = jnp.dot(normed, query_matrix, preferred_element_type=jnp.float32)]
    pallas_call x0 -> x8, Pallas kernels: none -> 9.99 us  [the longest x1 5.84 us: per_device(): pl.pallas_call(attend_kernel, in_specs=[IN_SMEM] + [IN_VMEM] * len(operan...]
    dot_general x4 -> x0, matrix products: 8.6 us -> none  [the longest x1 4.03 us: per_device(): queries = jnp.dot(normed, query_matrix, preferred_element_type=jnp.float32)]
    ppermute x1 -> x15, waiting for transfers between devices: 25 us -> 33 us  [the longest x3 19.2 us: send(): return lax.ppermute(value, ('segment', 'tp'), both)]
    unnamed x6 -> x8, local copies, waits for them, and re-layouts: 10.6 us -> 3.39 us
  transfers between devices with their start and end apart: 3 -> 15, of which waited for: 3 -> 8; matrix products, arithmetic and copies ran while one was open for 12% -> 2% of each run, Pallas kernels for 0% -> 4%
where the time goes in v2:
time: 71.4 us; the launch traced here: 71.2 us
  waiting for transfers between devices  33 us (46%)
  starting transfers between devices  21.6 us (30%)
  Pallas kernels  9.99 us (14%)
  local copies, waits for them, and re-layouts  5.71 us (8%)
  other arithmetic  0.76 us (1%)
    ppermute x3, waiting for transfers between devices, send(): return lax.ppermute(value, ('segment', 'tp'), both)  19.2 us
    ppermute x12, starting transfers between devices, send(): return lax.ppermute(value, 'tp', [pair[:2] for pair in pairs])  15.9 us
    ppermute x12, waiting for transfers between devices, send(): return lax.ppermute(value, 'tp', [pair[:2] for pair in pairs])  13.9 us
    pallas_call x1, Pallas kernels, per_device(): pl.pallas_call(attend_kernel, in_specs=[IN_SMEM] + [IN_VMEM] * len(operan...  5.84 us
    ppermute x3, starting transfers between devices, send(): return lax.ppermute(value, ('segment', 'tp'), both)  5.7 us
    unnamed x8, local copies, waits for them, and re-layouts  3.39 us
    pallas_call x1, Pallas kernels, fold_weights(): pl.pallas_call(weights_kernel, grid=(width // depth,), in_specs=[pl.Block...  2.74 us
    squeeze x1, local copies, waits for them, and re-layouts, block(): lax.dynamic_slice(blocks, (at_chip, at_core, 0, 0), (1, 1) + blocks.shape...  1.68 us
  transfers between devices with their start and end apart: 15, of which 8 were waited for; matrix products, arithmetic and copies ran while one was open for 2% of the time, Pallas kernels for 4%

profile of v2, /device:TPU:1, one launch (start us, length us, event | category | flops | bytes accessed | tf_op | source)
XLA Modules:
  0.0 71.2 jit_solution(3817212140976519868)
XLA Ops:
  0.0 1.7 %dynamic-slice_bitcast_fusion = (bf16[32,4096]{1,0:T(8,128)(2,1)S(1)}, bf16[32,4096]{1,0:T(8,128)(2,1)S(1)}, bf16[32,4096]{1,0:T(8,128)(2,1)S(1)}, bf16[32,4096]...) fusion(bf16[4,2,32,4096]{3,2,1,0:T(8,128)(2,1)} %bitcast.31, ...), kind=kLoop, calls=%fused_computation | loop fusion | bytes 4194328 | tf_op jit(solution)/shard_map/squeeze | solution.py:151
  1.7 0.0 copy-start.3
  1.7 3.3 %collective-permute-start.5 = (bf16[32,4096]{1,0:T(8,128)(2,1)S(1)}, bf16[32,4096]{1,0:T(8,128)(2,1)S(1)}, u32[]{:S(2)}, u32[]{:S(2)}) collective-permute-start(bf16[32,4096]{1,0:T(8,128)(2,1)S(1)} %get-tuple-element.11), channel_id=1, source_target_pairs={{0,1},{1,0},{2,3},{3,2},{4,5},{5,4},{6,7},{7,6},{8,9},{9,8},{10,11... | collective-permute-start | bytes 786440 | tf_op jit(solution)/shard_map/ppermute | solution.py:32
  5.0 0.1 collective-permute-start.2
  5.1 0.4 collective-permute-start
  5.5 0.1 collective-permute-start.4
  5.6 0.6 collective-permute-done.5.refs_1_
  6.2 0.1 shard_map.57
  6.3 4.4 %collective-permute-start.6 = (bf16[32,4096]{1,0:T(8,128)(2,1)S(1)}, bf16[32,4096]{1,0:T(8,128)(2,1)S(1)}, u32[]{:S(2)}, u32[]{:S(2)}) collective-permute-start(bf16[32,4096]{1,0:T(8,128)(2,1)S(1)} %shard_map.57), channel_id=1, source_target_pairs={{0,2},{1,7},{2,0},{3,5},{4,6},{5,3},{6,4},{7,1},{8,10},{9,15},{10,... | collective-permute-start | bytes 786440 | tf_op jit(solution)/shard_map/ppermute | solution.py:32
  10.6 0.0 collective-permute-done.2.refs_1_
  10.6 0.1 shard_map.56
  10.7 1.3 %collective-permute-start.3 = (bf16[32,4096]{1,0:T(8,128)(2,1)S(1)}, bf16[32,4096]{1,0:T(8,128)(2,1)S(1)}, u32[]{:S(2)}, u32[]{:S(2)}) collective-permute-start(bf16[32,4096]{1,0:T(8,128)(2,1)S(1)} %shard_map.56), channel_id=1, source_target_pairs={{0,10},{1,15},{2,8},{3,13},{4,14},{5,11},{6,12},{7,9},{8,18},{9,23... | collective-permute-start | bytes 786440 | tf_op jit(solution)/shard_map/ppermute | solution.py:34
  12.0 0.0 collective-permute-done.refs_1_
  12.0 0.0 copy-done.2
  12.0 0.1 shard_map.55
  12.1 1.4 %collective-permute-start.1 = (bf16[32,4096]{1,0:T(8,128)(2,1)S(1)}, bf16[32,4096]{1,0:T(8,128)(2,1)S(1)}, u32[]{:S(2)}, u32[]{:S(2)}) collective-permute-start(bf16[32,4096]{1,0:T(8,128)(2,1)S(1)} %shard_map.55), channel_id=1, source_target_pairs={{0,8},{1,9},{2,10},{3,11},{4,12},{5,13},{6,14},{7,15},{8,16},{9,17... | collective-permute-start | bytes 786440 | tf_op jit(solution)/shard_map/ppermute | solution.py:34
  13.5 0.0 collective-permute-done.4.refs_1_
  13.5 3.3 %collective-permute-done.6.refs_2_ = bf16[32,4096]{1,0:T(8,128)(2,1)S(1)} collective-permute-done((bf16[32,4096]{1,0:T(8,128)(2,1)S(1)}, bf16[32,4096]{1,0:T(8,128)(2,1)S(1)}, u32[]{:S(2)}, u32[]{:S(2)}) %collective-permute-start.6) | collective-permute-done | bytes 262176 | tf_op jit(solution)/shard_map/ppermute | solution.py:32
  16.8 0.1 shard_map.58
  16.9 3.0 %collective-permute-start.7 = (bf16[32,4096]{1,0:T(8,128)(2,1)S(1)}, bf16[32,4096]{1,0:T(8,128)(2,1)}, u32[]{:S(2)}, u32[]{:S(2)}) collective-permute-start(bf16[32,4096]{1,0:T(8,128)(2,1)S(1)} %shard_map.58), channel_id=1, source_target_pairs={{0,14},{1,11},{2,12},{3,9},{4,10},{5,15},{6,8},{7,13},{8,22},{9,19... | collective-permute-start | bytes 786440 | tf_op jit(solution)/shard_map/ppermute | solution.py:34
  19.9 0.0 copy-done.3
  19.9 0.6 copy.7.gain_ref
  20.5 0.0 copy-start.1
  20.6 7.0 %collective-permute-done.3.refs_1_ = bf16[32,4096]{1,0:T(8,128)(2,1)S(1)} collective-permute-done((bf16[32,4096]{1,0:T(8,128)(2,1)S(1)}, bf16[32,4096]{1,0:T(8,128)(2,1)S(1)}, u32[]{:S(2)}, u32[]{:S(2)}) %collective-permute-start.3) | collective-permute-done | bytes 262176 | tf_op jit(solution)/shard_map/ppermute | solution.py:34
  27.6 9.9 %collective-permute-done.1.refs_0_ = bf16[32,4096]{1,0:T(8,128)(2,1)S(1)} collective-permute-done((bf16[32,4096]{1,0:T(8,128)(2,1)S(1)}, bf16[32,4096]{1,0:T(8,128)(2,1)S(1)}, u32[]{:S(2)}, u32[]{:S(2)}) %collective-permute-start.1) | collective-permute-done | bytes 262176 | tf_op jit(solution)/shard_map/ppermute | solution.py:34
  37.5 2.3 %collective-permute-done.7.refs_2_ = bf16[32,4096]{1,0:T(8,128)(2,1)} collective-permute-done((bf16[32,4096]{1,0:T(8,128)(2,1)S(1)}, bf16[32,4096]{1,0:T(8,128)(2,1)}, u32[]{:S(2)}, u32[]{:S(2)}) %collective-permute-start.7) | collective-permute-done | bytes 262176 | tf_op jit(solution)/shard_map/ppermute | solution.py:34
  39.7 1.0 %shard_map.59.refs_0_ = bf16[32,4096]{1,0:T(8,128)(2,1)S(1)} custom-call(bf16[32,4096]{1,0:T(8,128)(2,1)S(1)} %collective-permute-done.1.refs_0_, bf16[32,4096]{1,0:T(8,128)(2,1)S(1)} %collective-permute-done.3.refs_1_, bf16[32,4096]{1,0:T(8,128)(2,1)} %collective-permute-done.7.refs_2_), custom_call_target="tpu_custom_call" | custom-call | tf_op jit(solution)/shard_map/pallas_call | solution.py:52
  40.8 0.1 collective-permute-start.9
  40.9 0.5 fusion
  41.4 0.1 pad_maximum_fusion
  41.6 0.0 copy-start
  41.6 3.4 %copy-done = bf16[1,4096,1,8,128]{4,3,2,1,0:T(8,128)(2,1)S(1)} copy-done((bf16[1,4096,1,8,128]{4,3,2,1,0:T(8,128)(2,1)S(1)}, bf16[1,4096,1,8,128]{4,3,2,1,0:T(8,128)(2,1)}, u32[]{:S(2)}) %copy-start) | copy-done | bytes 8388632
  45.0 2.7 %shard_map.60 = (bf16[4096,1024]{1,0:T(8,128)(2,1)S(1)}, bf16[4096,256]{1,0:T(8,128)(2,1)S(1)}) custom-call(bf16[4096,8,128]{2,1,0:T(8,128)(2,1)S(1)} %bitcast.28, bf16[4096,2,128]{2,1,0:T(2,128)(2,1)S(1)} %bitcast.29, f32[4096,1]{1,0:T(8,128)S(1)} %copy.7.gain_ref, bf16[32,4096]{1,0:T(8,128)(2,1)S(1)} %shard_map.59.refs_0_), custom_call_target="tpu_custom_call" | custom-call | bytes 20971520 | tf_op jit(solution)/shard_map/pallas_call | solution.py:75
  47.7 6.3 %collective-permute-start.11 = (bf16[32,4096]{1,0:T(8,128)(2,1)S(1)}, bf16[32,4096]{1,0:T(8,128)(2,1)S(1)}, u32[]{:S(2)}, u32[]{:S(2)}) collective-permute-start(bf16[32,4096]{1,0:T(8,128)(2,1)S(1)} %shard_map.61), channel_id=1, source_target_pairs={{0,2},{1,7},{2,0},{3,5},{4,6},{5,3},{6,4},{7,1},{8,10},{9,15},{10,... | collective-permute-start | bytes 786440 | tf_op jit(solution)/shard_map/ppermute | solution.py:32
  54.0 0.0 collective-permute-done.9.refs_2_
  54.0 0.1 collective-permute-start.13
  54.1 1.1 %collective-permute-start.8 = (bf16[32,4096]{1,0:T(8,128)(2,1)S(1)}, bf16[32,4096]{1,0:T(8,128)(2,1)S(1)}, u32[]{:S(2)}, u32[]{:S(2)}) collective-permute-start(bf16[32,4096]{1,0:T(8,128)(2,1)S(1)} %shard_map.59.refs_0_), channel_id=1, source_target_pairs={{0,1},{1,0},{2,3},{3,2},{4,5},{5,4},{6,7},{7,6},{8,9},{9,8},{10,11... | collective-permute-start | bytes 786440 | tf_op jit(solution)/shard_map/ppermute | solution.py:32
  55.2 0.0 collective-permute-start.10
  55.2 5.8 %collective-permute-done.11.refs_4_ = bf16[32,4096]{1,0:T(8,128)(2,1)S(1)} collective-permute-done((bf16[32,4096]{1,0:T(8,128)(2,1)S(1)}, bf16[32,4096]{1,0:T(8,128)(2,1)S(1)}, u32[]{:S(2)}, u32[]{:S(2)}) %collective-permute-start.11) | collective-permute-done | bytes 262176 | tf_op jit(solution)/shard_map/ppermute | solution.py:32
  61.0 0.0 collective-permute-start.12
  61.0 2.8 %collective-permute-done.13.refs_6_ = bf16[32,4096]{1,0:T(8,128)(2,1)S(1)} collective-permute-done((bf16[32,4096]{1,0:T(8,128)(2,1)S(1)}, bf16[32,4096]{1,0:T(8,128)(2,1)S(1)}, u32[]{:S(2)}, u32[]{:S(2)}) %collective-permute-start.13) | collective-permute-done | bytes 262176 | tf_op jit(solution)/shard_map/ppermute | solution.py:32
  63.8 0.0 collective-permute-start.14
  63.8 0.1 pad_add_fusion.place_ref
  63.9 0.0 collective-permute-done.8.refs_1_
  63.9 0.0 collective-permute-done.12.refs_5_
  63.9 0.0 collective-permute-done.10.refs_3_
  63.9 1.4 %collective-permute-done.14.refs_7_ = bf16[32,4096]{1,0:T(8,128)(2,1)S(1)} collective-permute-done((bf16[32,4096]{1,0:T(8,128)(2,1)S(1)}, bf16[32,4096]{1,0:T(8,128)(2,1)S(1)}, u32[]{:S(2)}, u32[]{:S(2)}) %collective-permute-start.14) | collective-permute-done | bytes 262176 | tf_op jit(solution)/shard_map/ppermute | solution.py:32
  65.4 5.8 %shard_map.62 = bf16[256,8,128]{2,1,0:T(8,128)(2,1)} custom-call(s32[4]{0:T(128)S(1)} %pad_add_fusion.place_ref, bf16[32,4096]{1,0:T(8,128)(2,1)S(1)} %shard_map.59.refs_0_, bf16[32,4096]{1,0:T(8,128)(2,1)S(1)} %collective-permute-done.8.refs_1_, bf16[32,4096]{1,0:T(8,128)(2,1)S(1)} %collective-permute-done.9.refs_2_, ...), custom_call_target="tpu_custom_call" | custom-call | flops 2684354560 | bytes 14680064 | tf_op jit(solution)/shard_map/pallas_call | solution.py:182
  (5 shorter events, 0.0 us)
Async XLA Ops:
  0.0 12.0 %copy-start.2 = (bf16[1,32,4096]{2,1,0:T(8,128)(2,1)S(1)}, bf16[1,32,4096]{2,1,0:T(8,128)(2,1)}, u32[]{:S(2)}) copy-start(bf16[1,32,4096]{2,1,0:T(8,128)(2,1)} %param.6) | copy-start | bytes 786436
  1.7 18.2 %copy-start.3 = (f32[1,4096]{1,0:T(1,128)S(1)}, f32[1,4096]{1,0:T(1,128)}, u32[]{:S(2)}) copy-start(f32[1,4096]{1,0:T(1,128)} %param.7) | copy-start | bytes 49156
  1.7 4.5 %collective-permute-start.5 = (bf16[32,4096]{1,0:T(8,128)(2,1)S(1)}, bf16[32,4096]{1,0:T(8,128)(2,1)S(1)}, u32[]{:S(2)}, u32[]{:S(2)}) collective-permute-start(bf16[32,4096]{1,0:T(8,128)(2,1)S(1)} %get-tuple-element.11), channel_id=1, source_target_pairs={{0,1},{1,0},{2,3},{3,2},{4,5},{5,4},{6,7},{7,6},{8,9},{9,8},{10,11... | collective-permute-start | bytes 786440 | tf_op jit(solution)/shard_map/ppermute | solution.py:32
  5.0 5.6 %collective-permute-start.2 = (bf16[32,4096]{1,0:T(8,128)(2,1)S(1)}, bf16[32,4096]{1,0:T(8,128)(2,1)S(1)}, u32[]{:S(2)}, u32[]{:S(2)}) collective-permute-start(bf16[32,4096]{1,0:T(8,128)(2,1)S(1)} %get-tuple-element.15), channel_id=1, source_target_pairs={{0,1},{1,0},{2,3},{3,2},{4,5},{5,4},{6,7},{7,6},{8,9},{9,8},{10,11... | collective-permute-start | bytes 786440 | tf_op jit(solution)/shard_map/ppermute | solution.py:32
  5.1 6.9 %collective-permute-start = (bf16[32,4096]{1,0:T(8,128)(2,1)S(1)}, bf16[32,4096]{1,0:T(8,128)(2,1)S(1)}, u32[]{:S(2)}, u32[]{:S(2)}) collective-permute-start(bf16[32,4096]{1,0:T(8,128)(2,1)S(1)} %get-tuple-element.17), channel_id=1, source_target_pairs={{0,1},{1,0},{2,3},{3,2},{4,5},{5,4},{6,7},{7,6},{8,9},{9,8},{10,11... | collective-permute-start | bytes 786440 | tf_op jit(solution)/shard_map/ppermute | solution.py:32
  5.5 8.0 %collective-permute-start.4 = (bf16[32,4096]{1,0:T(8,128)(2,1)S(1)}, bf16[32,4096]{1,0:T(8,128)(2,1)S(1)}, u32[]{:S(2)}, u32[]{:S(2)}) collective-permute-start(bf16[32,4096]{1,0:T(8,128)(2,1)S(1)} %get-tuple-element.13), channel_id=1, source_target_pairs={{0,1},{1,0},{2,3},{3,2},{4,5},{5,4},{6,7},{7,6},{8,9},{9,8},{10,11... | collective-permute-start | bytes 786440 | tf_op jit(solution)/shard_map/ppermute | solution.py:32
  6.3 10.5 %collective-permute-start.6 = (bf16[32,4096]{1,0:T(8,128)(2,1)S(1)}, bf16[32,4096]{1,0:T(8,128)(2,1)S(1)}, u32[]{:S(2)}, u32[]{:S(2)}) collective-permute-start(bf16[32,4096]{1,0:T(8,128)(2,1)S(1)} %shard_map.57), channel_id=1, source_target_pairs={{0,2},{1,7},{2,0},{3,5},{4,6},{5,3},{6,4},{7,1},{8,10},{9,15},{10,... | collective-permute-start | bytes 786440 | tf_op jit(solution)/shard_map/ppermute | solution.py:32
  10.7 16.9 %collective-permute-start.3 = (bf16[32,4096]{1,0:T(8,128)(2,1)S(1)}, bf16[32,4096]{1,0:T(8,128)(2,1)S(1)}, u32[]{:S(2)}, u32[]{:S(2)}) collective-permute-start(bf16[32,4096]{1,0:T(8,128)(2,1)S(1)} %shard_map.56), channel_id=1, source_target_pairs={{0,10},{1,15},{2,8},{3,13},{4,14},{5,11},{6,12},{7,9},{8,18},{9,23... | collective-permute-start | bytes 786440 | tf_op jit(solution)/shard_map/ppermute | solution.py:34
  12.1 25.3 %collective-permute-start.1 = (bf16[32,4096]{1,0:T(8,128)(2,1)S(1)}, bf16[32,4096]{1,0:T(8,128)(2,1)S(1)}, u32[]{:S(2)}, u32[]{:S(2)}) collective-permute-start(bf16[32,4096]{1,0:T(8,128)(2,1)S(1)} %shard_map.55), channel_id=1, source_target_pairs={{0,8},{1,9},{2,10},{3,11},{4,12},{5,13},{6,14},{7,15},{8,16},{9,17... | collective-permute-start | bytes 786440 | tf_op jit(solution)/shard_map/ppermute | solution.py:34
  16.9 22.9 %collective-permute-start.7 = (bf16[32,4096]{1,0:T(8,128)(2,1)S(1)}, bf16[32,4096]{1,0:T(8,128)(2,1)}, u32[]{:S(2)}, u32[]{:S(2)}) collective-permute-start(bf16[32,4096]{1,0:T(8,128)(2,1)S(1)} %shard_map.58), channel_id=1, source_target_pairs={{0,14},{1,11},{2,12},{3,9},{4,10},{5,15},{6,8},{7,13},{8,22},{9,19... | collective-permute-start | bytes 786440 | tf_op jit(solution)/shard_map/ppermute | solution.py:34
  20.5 21.0 %copy-start.1 = (bf16[1,4096,1,2,128]{4,3,2,1,0:T(2,128)(2,1)S(1)}, bf16[1,4096,1,2,128]{4,3,2,1,0:T(2,128)(2,1)}, u32[]{:S(2)}) copy-start(bf16[1,4096,1,2,128]{4,3,2,1,0:T(2,128)(2,1)} %param.9) | copy-start | bytes 6291460
  40.8 13.2 %collective-permute-start.9 = (bf16[32,4096]{1,0:T(8,128)(2,1)S(1)}, bf16[32,4096]{1,0:T(8,128)(2,1)S(1)}, u32[]{:S(2)}, u32[]{:S(2)}) collective-permute-start(bf16[32,4096]{1,0:T(8,128)(2,1)S(1)} %shard_map.59.refs_0_), channel_id=1, source_target_pairs={{0,6},{1,3},{2,4},{3,1},{4,2},{5,7},{6,0},{7,5},{8,14},{9,11},{10,... | collective-permute-start | bytes 786440 | tf_op jit(solution)/shard_map/ppermute | solution.py:32
  41.6 3.4 %copy-start = (bf16[1,4096,1,8,128]{4,3,2,1,0:T(8,128)(2,1)S(1)}, bf16[1,4096,1,8,128]{4,3,2,1,0:T(8,128)(2,1)}, u32[]{:S(2)}) copy-start(bf16[1,4096,1,8,128]{4,3,2,1,0:T(8,128)(2,1)} %param.8) | copy-start | bytes 25165828
  47.7 13.3 %collective-permute-start.11 = (bf16[32,4096]{1,0:T(8,128)(2,1)S(1)}, bf16[32,4096]{1,0:T(8,128)(2,1)S(1)}, u32[]{:S(2)}, u32[]{:S(2)}) collective-permute-start(bf16[32,4096]{1,0:T(8,128)(2,1)S(1)} %shard_map.61), channel_id=1, source_target_pairs={{0,2},{1,7},{2,0},{3,5},{4,6},{5,3},{6,4},{7,1},{8,10},{9,15},{10,... | collective-permute-start | bytes 786440 | tf_op jit(solution)/shard_map/ppermute | solution.py:32
  54.0 9.8 %collective-permute-start.13 = (bf16[32,4096]{1,0:T(8,128)(2,1)S(1)}, bf16[32,4096]{1,0:T(8,128)(2,1)S(1)}, u32[]{:S(2)}, u32[]{:S(2)}) collective-permute-start(bf16[32,4096]{1,0:T(8,128)(2,1)S(1)} %collective-permute-done.9.refs_2_), channel_id=1, source_target_pairs={{0,2},{1,7},{2,0},{3,5},{4,6},{5,3},{6,4},{7,1},{8,10},{9,15},{10,... | collective-permute-start | bytes 786440 | tf_op jit(solution)/shard_map/ppermute | solution.py:32
  54.1 9.8 %collective-permute-start.8 = (bf16[32,4096]{1,0:T(8,128)(2,1)S(1)}, bf16[32,4096]{1,0:T(8,128)(2,1)S(1)}, u32[]{:S(2)}, u32[]{:S(2)}) collective-permute-start(bf16[32,4096]{1,0:T(8,128)(2,1)S(1)} %shard_map.59.refs_0_), channel_id=1, source_target_pairs={{0,1},{1,0},{2,3},{3,2},{4,5},{5,4},{6,7},{7,6},{8,9},{9,8},{10,11... | collective-permute-start | bytes 786440 | tf_op jit(solution)/shard_map/ppermute | solution.py:32
  55.2 8.7 %collective-permute-start.10 = (bf16[32,4096]{1,0:T(8,128)(2,1)S(1)}, bf16[32,4096]{1,0:T(8,128)(2,1)S(1)}, u32[]{:S(2)}, u32[]{:S(2)}) collective-permute-start(bf16[32,4096]{1,0:T(8,128)(2,1)S(1)} %collective-permute-done.9.refs_2_), channel_id=1, source_target_pairs={{0,1},{1,0},{2,3},{3,2},{4,5},{5,4},{6,7},{7,6},{8,9},{9,8},{10,11... | collective-permute-start | bytes 786440 | tf_op jit(solution)/shard_map/ppermute | solution.py:32
  61.0 2.9 %collective-permute-start.12 = (bf16[32,4096]{1,0:T(8,128)(2,1)S(1)}, bf16[32,4096]{1,0:T(8,128)(2,1)S(1)}, u32[]{:S(2)}, u32[]{:S(2)}) collective-permute-start(bf16[32,4096]{1,0:T(8,128)(2,1)S(1)} %collective-permute-done.11.refs_4_), channel_id=1, source_target_pairs={{0,1},{1,0},{2,3},{3,2},{4,5},{5,4},{6,7},{7,6},{8,9},{9,8},{10,11... | collective-permute-start | bytes 786440 | tf_op jit(solution)/shard_map/ppermute | solution.py:32
  63.8 1.5 %collective-permute-start.14 = (bf16[32,4096]{1,0:T(8,128)(2,1)S(1)}, bf16[32,4096]{1,0:T(8,128)(2,1)S(1)}, u32[]{:S(2)}, u32[]{:S(2)}) collective-permute-start(bf16[32,4096]{1,0:T(8,128)(2,1)S(1)} %collective-permute-done.13.refs_6_), channel_id=1, source_target_pairs={{0,1},{1,0},{2,3},{3,2},{4,5},{5,4},{6,7},{7,6},{8,9},{9,8},{10,11... | collective-permute-start | bytes 786440 | tf_op jit(solution)/shard_map/ppermute | solution.py:32

commit v3 on v2

--- a/solution.py
+++ b/solution.py
@@ -156,10 +156,10 @@
     far_mine, one_mine, two_mine, here_mine = (block(at, core) for at in (chip ^ 2, one, two, chip))
     far_out = sum_after((far_mine, far_in))
     far = send(far_out, step=0)
-    here = send(sum_after((here_mine, here_in, residual[0])), sections=(1, 1))
-    near = send(sum_after((one_mine, one_in)), step=0, sections=(1, 1))
+    near = send(sum_after((one_mine, one_in)), step=0)
     last = send(sum_after((two_mine, two_in, far)), step=1, sections=(1, 1))
-    made = sum_after((here, near, last))
+    here = send(sum_after((here_mine, here_in, near, residual[0])), sections=(1, 1))
+    made = sum_after((here, last))
 
     half = head_dim // 2
     frequency = ROPE_BASE ** (-jnp.arange(half, dtype=jnp.float32) * 2.0 / head_dim)

time: 71.4 us -> 70.2 us (0.983)
  waiting for transfers between devices: 33 us -> 28.9 us
  starting transfers between devices: 21.6 us -> 25.4 us
  Pallas kernels: 9.99 us -> 9.05 us
    ppermute x3 -> x2, waiting for transfers between devices: 19.2 us -> 14.7 us  [send(): return lax.ppermute(value, ('segment', 'tp'), both)]
    ppermute x12 -> x13, starting transfers between devices: 15.9 us -> 18.3 us  [send(): return lax.ppermute(value, 'tp', [pair[:2] for pair in pairs])]
    ppermute x3 -> x2, starting transfers between devices: 5.7 us -> 7.17 us  [send(): return lax.ppermute(value, ('segment', 'tp'), both)]
    pallas_call x6, Pallas kernels: 1.4 us -> 0.47 us  [sum_after(): pl.pallas_call(functools.partial(sum_kernel, len(terms)), in_specs=[IN_VM...]
    ppermute x12 -> x13, waiting for transfers between devices: 13.9 us -> 14.2 us  [send(): return lax.ppermute(value, 'tp', [pair[:2] for pair in pairs])]
  transfers between devices with their start and end apart: 15 -> 15, of which waited for: 8 -> 8; matrix products, arithmetic and copies ran while one was open for 2% -> 2% of each run, Pallas kernels for 4% -> 5%
where the time goes in v3:
time: 70.2 us; the launch traced here: 69.9 us
  waiting for transfers between devices  28.9 us (41%)
  starting transfers between devices  25.4 us (36%)
  Pallas kernels  9.05 us (13%)
  local copies, waits for them, and re-layouts  5.68 us (8%)
  other arithmetic  0.76 us (1%)
    ppermute x13, starting transfers between devices, send(): return lax.ppermute(value, 'tp', [pair[:2] for pair in pairs])  18.3 us
    ppermute x2, waiting for transfers between devices, send(): return lax.ppermute(value, ('segment', 'tp'), both)  14.7 us
    ppermute x13, waiting for transfers between devices, send(): return lax.ppermute(value, 'tp', [pair[:2] for pair in pairs])  14.2 us
    ppermute x2, starting transfers between devices, send(): return lax.ppermute(value, ('segment', 'tp'), both)  7.17 us
    pallas_call x1, Pallas kernels, per_device(): pl.pallas_call(attend_kernel, in_specs=[IN_SMEM] + [IN_VMEM] * len(operan...  5.83 us
    unnamed x8, local copies, waits for them, and re-layouts  3.4 us
    pallas_call x1, Pallas kernels, fold_weights(): pl.pallas_call(weights_kernel, grid=(width // depth,), in_specs=[pl.Block...  2.74 us
    squeeze x1, local copies, waits for them, and re-layouts, block(): lax.dynamic_slice(blocks, (at_chip, at_core, 0, 0), (1, 1) + blocks.shape...  1.64 us
  transfers between devices with their start and end apart: 15, of which 8 were waited for; matrix products, arithmetic and copies ran while one was open for 2% of the time, Pallas kernels for 5%

profile of v3, /device:TPU:1, one launch (start us, length us, event | category | flops | bytes accessed | tf_op | source)
XLA Modules:
  0.0 69.9 jit_solution(6354334455877188250)
XLA Ops:
  0.0 1.6 %dynamic-slice_bitcast_fusion = (bf16[32,4096]{1,0:T(8,128)(2,1)S(1)}, bf16[32,4096]{1,0:T(8,128)(2,1)S(1)}, bf16[32,4096]{1,0:T(8,128)(2,1)S(1)}, bf16[32,4096]...) fusion(bf16[4,2,32,4096]{3,2,1,0:T(8,128)(2,1)} %bitcast.31, ...), kind=kLoop, calls=%fused_computation | loop fusion | bytes 4194328 | tf_op jit(solution)/shard_map/squeeze | solution.py:151
  1.6 0.0 copy-start.2
  1.7 0.0 copy-start.3
  1.7 3.3 %collective-permute-start.5 = (bf16[32,4096]{1,0:T(8,128)(2,1)S(1)}, bf16[32,4096]{1,0:T(8,128)(2,1)S(1)}, u32[]{:S(2)}, u32[]{:S(2)}) collective-permute-start(bf16[32,4096]{1,0:T(8,128)(2,1)S(1)} %get-tuple-element.11), channel_id=1, source_target_pairs={{0,1},{1,0},{2,3},{3,2},{4,5},{5,4},{6,7},{7,6},{8,9},{9,8},{10,11... | collective-permute-start | bytes 786440 | tf_op jit(solution)/shard_map/ppermute | solution.py:32
  5.0 0.1 collective-permute-start.1
  5.1 0.4 collective-permute-start.4
  5.5 0.7 collective-permute-done.5.refs_1_
  6.2 0.1 shard_map.57
  6.2 4.4 %collective-permute-start.6 = (bf16[32,4096]{1,0:T(8,128)(2,1)S(1)}, bf16[32,4096]{1,0:T(8,128)(2,1)S(1)}, u32[]{:S(2)}, u32[]{:S(2)}) collective-permute-start(bf16[32,4096]{1,0:T(8,128)(2,1)S(1)} %shard_map.57), channel_id=1, source_target_pairs={{0,2},{1,7},{2,0},{3,5},{4,6},{5,3},{6,4},{7,1},{8,10},{9,15},{10,... | collective-permute-start | bytes 786440 | tf_op jit(solution)/shard_map/ppermute | solution.py:32
  10.6 0.0 collective-permute-start
  10.6 0.0 collective-permute-done.1.refs_1_
  10.6 0.1 shard_map.55
  10.7 1.9 %collective-permute-start.2 = (bf16[32,4096]{1,0:T(8,128)(2,1)S(1)}, bf16[32,4096]{1,0:T(8,128)(2,1)S(1)}, u32[]{:S(2)}, u32[]{:S(2)}) collective-permute-start(bf16[32,4096]{1,0:T(8,128)(2,1)S(1)} %shard_map.55), channel_id=1, source_target_pairs={{0,2},{1,7},{2,0},{3,5},{4,6},{5,3},{6,4},{7,1},{8,10},{9,15},{10,... | collective-permute-start | bytes 786440 | tf_op jit(solution)/shard_map/ppermute | solution.py:32
  12.6 0.0 collective-permute-done.4.refs_1_
  12.6 2.5 %collective-permute-done.6.refs_2_ = bf16[32,4096]{1,0:T(8,128)(2,1)S(1)} collective-permute-done((bf16[32,4096]{1,0:T(8,128)(2,1)S(1)}, bf16[32,4096]{1,0:T(8,128)(2,1)S(1)}, u32[]{:S(2)}, u32[]{:S(2)}) %collective-permute-start.6) | collective-permute-done | bytes 262176 | tf_op jit(solution)/shard_map/ppermute | solution.py:32
  15.1 0.1 shard_map.58
  15.2 5.7 %collective-permute-start.7 = (bf16[32,4096]{1,0:T(8,128)(2,1)S(1)}, bf16[32,4096]{1,0:T(8,128)(2,1)S(1)}, u32[]{:S(2)}, u32[]{:S(2)}) collective-permute-start(bf16[32,4096]{1,0:T(8,128)(2,1)S(1)} %shard_map.58), channel_id=1, source_target_pairs={{0,14},{1,11},{2,12},{3,9},{4,10},{5,15},{6,8},{7,13},{8,22},{9,19... | collective-permute-start | bytes 786440 | tf_op jit(solution)/shard_map/ppermute | solution.py:34
  20.9 0.0 collective-permute-done.refs_1_
  20.9 0.9 %collective-permute-done.2.refs_2_ = bf16[32,4096]{1,0:T(8,128)(2,1)S(1)} collective-permute-done((bf16[32,4096]{1,0:T(8,128)(2,1)S(1)}, bf16[32,4096]{1,0:T(8,128)(2,1)S(1)}, u32[]{:S(2)}, u32[]{:S(2)}) %collective-permute-start.2) | collective-permute-done | bytes 262176 | tf_op jit(solution)/shard_map/ppermute | solution.py:32
  21.8 0.1 shard_map.56
  21.9 1.4 %collective-permute-start.3 = (bf16[32,4096]{1,0:T(8,128)(2,1)S(1)}, bf16[32,4096]{1,0:T(8,128)(2,1)S(1)}, u32[]{:S(2)}, u32[]{:S(2)}) collective-permute-start(bf16[32,4096]{1,0:T(8,128)(2,1)S(1)} %shard_map.56), channel_id=1, source_target_pairs={{0,8},{1,9},{2,10},{3,11},{4,12},{5,13},{6,14},{7,15},{8,16},{9,17... | collective-permute-start | bytes 786440 | tf_op jit(solution)/shard_map/ppermute | solution.py:34
  23.4 0.6 copy.7.gain_ref
  24.0 0.0 copy-start.1
  24.1 10.6 %collective-permute-done.7.refs_1_ = bf16[32,4096]{1,0:T(8,128)(2,1)S(1)} collective-permute-done((bf16[32,4096]{1,0:T(8,128)(2,1)S(1)}, bf16[32,4096]{1,0:T(8,128)(2,1)S(1)}, u32[]{:S(2)}, u32[]{:S(2)}) %collective-permute-start.7) | collective-permute-done | bytes 262176 | tf_op jit(solution)/shard_map/ppermute | solution.py:34
  34.6 4.1 %collective-permute-done.3.refs_0_ = bf16[32,4096]{1,0:T(8,128)(2,1)S(1)} collective-permute-done((bf16[32,4096]{1,0:T(8,128)(2,1)S(1)}, bf16[32,4096]{1,0:T(8,128)(2,1)S(1)}, u32[]{:S(2)}, u32[]{:S(2)}) %collective-permute-start.3) | collective-permute-done | bytes 262176 | tf_op jit(solution)/shard_map/ppermute | solution.py:34
  38.8 0.1 shard_map.59.refs_0_
  38.8 0.6 collective-permute-start.9
  39.4 0.5 fusion
  40.0 0.1 pad_maximum_fusion
  40.1 0.0 copy-done.1
  40.1 0.0 copy-start
  40.1 3.4 %copy-done = bf16[1,4096,1,8,128]{4,3,2,1,0:T(8,128)(2,1)S(1)} copy-done((bf16[1,4096,1,8,128]{4,3,2,1,0:T(8,128)(2,1)S(1)}, bf16[1,4096,1,8,128]{4,3,2,1,0:T(8,128)(2,1)}, u32[]{:S(2)}) %copy-start) | copy-done | bytes 8388632
  43.5 2.7 %shard_map.60 = (bf16[4096,1024]{1,0:T(8,128)(2,1)S(1)}, bf16[4096,256]{1,0:T(8,128)(2,1)S(1)}) custom-call(bf16[4096,8,128]{2,1,0:T(8,128)(2,1)S(1)} %bitcast.28, bf16[4096,2,128]{2,1,0:T(2,128)(2,1)S(1)} %bitcast.29, f32[4096,1]{1,0:T(8,128)S(1)} %copy.7.gain_ref, bf16[32,4096]{1,0:T(8,128)(2,1)S(1)} %shard_map.59.refs_0_), custom_call_target="tpu_custom_call" | custom-call | bytes 20971520 | tf_op jit(solution)/shard_map/pallas_call | solution.py:75
  46.3 4.1 %collective-permute-start.11 = (bf16[32,4096]{1,0:T(8,128)(2,1)S(1)}, bf16[32,4096]{1,0:T(8,128)(2,1)S(1)}, u32[]{:S(2)}, u32[]{:S(2)}) collective-permute-start(bf16[32,4096]{1,0:T(8,128)(2,1)S(1)} %shard_map.61), channel_id=1, source_target_pairs={{0,2},{1,7},{2,0},{3,5},{4,6},{5,3},{6,4},{7,1},{8,10},{9,15},{10,... | collective-permute-start | bytes 786440 | tf_op jit(solution)/shard_map/ppermute | solution.py:32
  50.4 0.0 collective-permute-done.9.refs_2_
  50.4 0.1 collective-permute-start.13
  50.5 2.3 %collective-permute-start.8 = (bf16[32,4096]{1,0:T(8,128)(2,1)S(1)}, bf16[32,4096]{1,0:T(8,128)(2,1)S(1)}, u32[]{:S(2)}, u32[]{:S(2)}) collective-permute-start(bf16[32,4096]{1,0:T(8,128)(2,1)S(1)} %shard_map.59.refs_0_), channel_id=1, source_target_pairs={{0,1},{1,0},{2,3},{3,2},{4,5},{5,4},{6,7},{7,6},{8,9},{9,8},{10,11... | collective-permute-start | bytes 786440 | tf_op jit(solution)/shard_map/ppermute | solution.py:32
  52.8 0.0 collective-permute-start.10
  52.8 6.8 %collective-permute-done.11.refs_4_ = bf16[32,4096]{1,0:T(8,128)(2,1)S(1)} collective-permute-done((bf16[32,4096]{1,0:T(8,128)(2,1)S(1)}, bf16[32,4096]{1,0:T(8,128)(2,1)S(1)}, u32[]{:S(2)}, u32[]{:S(2)}) %collective-permute-start.11) | collective-permute-done | bytes 262176 | tf_op jit(solution)/shard_map/ppermute | solution.py:32
  59.6 0.5 collective-permute-start.12
  60.1 2.3 %collective-permute-done.13.refs_6_ = bf16[32,4096]{1,0:T(8,128)(2,1)S(1)} collective-permute-done((bf16[32,4096]{1,0:T(8,128)(2,1)S(1)}, bf16[32,4096]{1,0:T(8,128)(2,1)S(1)}, u32[]{:S(2)}, u32[]{:S(2)}) %collective-permute-start.13) | collective-permute-done | bytes 262176 | tf_op jit(solution)/shard_map/ppermute | solution.py:32
  62.4 0.5 collective-permute-start.14
  62.9 0.1 pad_add_fusion.place_ref
  63.0 0.0 collective-permute-done.8.refs_1_
  63.0 0.0 collective-permute-done.12.refs_5_
  63.0 0.0 collective-permute-done.10.refs_3_
  63.0 1.1 %collective-permute-done.14.refs_7_ = bf16[32,4096]{1,0:T(8,128)(2,1)S(1)} collective-permute-done((bf16[32,4096]{1,0:T(8,128)(2,1)S(1)}, bf16[32,4096]{1,0:T(8,128)(2,1)S(1)}, u32[]{:S(2)}, u32[]{:S(2)}) %collective-permute-start.14) | collective-permute-done | bytes 262176 | tf_op jit(solution)/shard_map/ppermute | solution.py:32
  64.1 5.8 %shard_map.62 = bf16[256,8,128]{2,1,0:T(8,128)(2,1)} custom-call(s32[4]{0:T(128)S(1)} %pad_add_fusion.place_ref, bf16[32,4096]{1,0:T(8,128)(2,1)S(1)} %shard_map.59.refs_0_, bf16[32,4096]{1,0:T(8,128)(2,1)S(1)} %collective-permute-done.8.refs_1_, bf16[32,4096]{1,0:T(8,128)(2,1)S(1)} %collective-permute-done.9.refs_2_, ...), custom_call_target="tpu_custom_call" | custom-call | flops 2684354560 | bytes 14680064 | tf_op jit(solution)/shard_map/pallas_call | solution.py:182
  (5 shorter events, 0.0 us)
Async XLA Ops:
  1.6 20.1 %copy-start.2 = (bf16[1,32,4096]{2,1,0:T(8,128)(2,1)S(1)}, bf16[1,32,4096]{2,1,0:T(8,128)(2,1)}, u32[]{:S(2)}) copy-start(bf16[1,32,4096]{2,1,0:T(8,128)(2,1)} %param.6) | copy-start | bytes 786436
  1.7 21.7 %copy-start.3 = (f32[1,4096]{1,0:T(1,128)S(1)}, f32[1,4096]{1,0:T(1,128)}, u32[]{:S(2)}) copy-start(f32[1,4096]{1,0:T(1,128)} %param.7) | copy-start | bytes 49156
  1.7 4.5 %collective-permute-start.5 = (bf16[32,4096]{1,0:T(8,128)(2,1)S(1)}, bf16[32,4096]{1,0:T(8,128)(2,1)S(1)}, u32[]{:S(2)}, u32[]{:S(2)}) collective-permute-start(bf16[32,4096]{1,0:T(8,128)(2,1)S(1)} %get-tuple-element.11), channel_id=1, source_target_pairs={{0,1},{1,0},{2,3},{3,2},{4,5},{5,4},{6,7},{7,6},{8,9},{9,8},{10,11... | collective-permute-start | bytes 786440 | tf_op jit(solution)/shard_map/ppermute | solution.py:32
  5.0 5.6 %collective-permute-start.1 = (bf16[32,4096]{1,0:T(8,128)(2,1)S(1)}, bf16[32,4096]{1,0:T(8,128)(2,1)S(1)}, u32[]{:S(2)}, u32[]{:S(2)}) collective-permute-start(bf16[32,4096]{1,0:T(8,128)(2,1)S(1)} %get-tuple-element.15), channel_id=1, source_target_pairs={{0,1},{1,0},{2,3},{3,2},{4,5},{5,4},{6,7},{7,6},{8,9},{9,8},{10,11... | collective-permute-start | bytes 786440 | tf_op jit(solution)/shard_map/ppermute | solution.py:32
  5.1 7.5 %collective-permute-start.4 = (bf16[32,4096]{1,0:T(8,128)(2,1)S(1)}, bf16[32,4096]{1,0:T(8,128)(2,1)S(1)}, u32[]{:S(2)}, u32[]{:S(2)}) collective-permute-start(bf16[32,4096]{1,0:T(8,128)(2,1)S(1)} %get-tuple-element.13), channel_id=1, source_target_pairs={{0,1},{1,0},{2,3},{3,2},{4,5},{5,4},{6,7},{7,6},{8,9},{9,8},{10,11... | collective-permute-start | bytes 786440 | tf_op jit(solution)/shard_map/ppermute | solution.py:32
  6.2 8.8 %collective-permute-start.6 = (bf16[32,4096]{1,0:T(8,128)(2,1)S(1)}, bf16[32,4096]{1,0:T(8,128)(2,1)S(1)}, u32[]{:S(2)}, u32[]{:S(2)}) collective-permute-start(bf16[32,4096]{1,0:T(8,128)(2,1)S(1)} %shard_map.57), channel_id=1, source_target_pairs={{0,2},{1,7},{2,0},{3,5},{4,6},{5,3},{6,4},{7,1},{8,10},{9,15},{10,... | collective-permute-start | bytes 786440 | tf_op jit(solution)/shard_map/ppermute | solution.py:32
  10.6 10.3 %collective-permute-start = (bf16[32,4096]{1,0:T(8,128)(2,1)S(1)}, bf16[32,4096]{1,0:T(8,128)(2,1)S(1)}, u32[]{:S(2)}, u32[]{:S(2)}) collective-permute-start(bf16[32,4096]{1,0:T(8,128)(2,1)S(1)} %get-tuple-element.17), channel_id=1, source_target_pairs={{0,1},{1,0},{2,3},{3,2},{4,5},{5,4},{6,7},{7,6},{8,9},{9,8},{10,11... | collective-permute-start | bytes 786440 | tf_op jit(solution)/shard_map/ppermute | solution.py:32
  10.7 11.1 %collective-permute-start.2 = (bf16[32,4096]{1,0:T(8,128)(2,1)S(1)}, bf16[32,4096]{1,0:T(8,128)(2,1)S(1)}, u32[]{:S(2)}, u32[]{:S(2)}) collective-permute-start(bf16[32,4096]{1,0:T(8,128)(2,1)S(1)} %shard_map.55), channel_id=1, source_target_pairs={{0,2},{1,7},{2,0},{3,5},{4,6},{5,3},{6,4},{7,1},{8,10},{9,15},{10,... | collective-permute-start | bytes 786440 | tf_op jit(solution)/shard_map/ppermute | solution.py:32
  15.2 19.4 %collective-permute-start.7 = (bf16[32,4096]{1,0:T(8,128)(2,1)S(1)}, bf16[32,4096]{1,0:T(8,128)(2,1)S(1)}, u32[]{:S(2)}, u32[]{:S(2)}) collective-permute-start(bf16[32,4096]{1,0:T(8,128)(2,1)S(1)} %shard_map.58), channel_id=1, source_target_pairs={{0,14},{1,11},{2,12},{3,9},{4,10},{5,15},{6,8},{7,13},{8,22},{9,19... | collective-permute-start | bytes 786440 | tf_op jit(solution)/shard_map/ppermute | solution.py:34
  21.9 16.8 %collective-permute-start.3 = (bf16[32,4096]{1,0:T(8,128)(2,1)S(1)}, bf16[32,4096]{1,0:T(8,128)(2,1)S(1)}, u32[]{:S(2)}, u32[]{:S(2)}) collective-permute-start(bf16[32,4096]{1,0:T(8,128)(2,1)S(1)} %shard_map.56), channel_id=1, source_target_pairs={{0,8},{1,9},{2,10},{3,11},{4,12},{5,13},{6,14},{7,15},{8,16},{9,17... | collective-permute-start | bytes 786440 | tf_op jit(solution)/shard_map/ppermute | solution.py:34
  24.0 16.1 %copy-start.1 = (bf16[1,4096,1,2,128]{4,3,2,1,0:T(2,128)(2,1)S(1)}, bf16[1,4096,1,2,128]{4,3,2,1,0:T(2,128)(2,1)}, u32[]{:S(2)}) copy-start(bf16[1,4096,1,2,128]{4,3,2,1,0:T(2,128)(2,1)} %param.9) | copy-start | bytes 6291460
  38.8 11.6 %collective-permute-start.9 = (bf16[32,4096]{1,0:T(8,128)(2,1)S(1)}, bf16[32,4096]{1,0:T(8,128)(2,1)S(1)}, u32[]{:S(2)}, u32[]{:S(2)}) collective-permute-start(bf16[32,4096]{1,0:T(8,128)(2,1)S(1)} %shard_map.59.refs_0_), channel_id=1, source_target_pairs={{0,6},{1,3},{2,4},{3,1},{4,2},{5,7},{6,0},{7,5},{8,14},{9,11},{10,... | collective-permute-start | bytes 786440 | tf_op jit(solution)/shard_map/ppermute | solution.py:32
  40.1 3.4 %copy-start = (bf16[1,4096,1,8,128]{4,3,2,1,0:T(8,128)(2,1)S(1)}, bf16[1,4096,1,8,128]{4,3,2,1,0:T(8,128)(2,1)}, u32[]{:S(2)}) copy-start(bf16[1,4096,1,8,128]{4,3,2,1,0:T(8,128)(2,1)} %param.8) | copy-start | bytes 25165828
  46.3 13.3 %collective-permute-start.11 = (bf16[32,4096]{1,0:T(8,128)(2,1)S(1)}, bf16[32,4096]{1,0:T(8,128)(2,1)S(1)}, u32[]{:S(2)}, u32[]{:S(2)}) collective-permute-start(bf16[32,4096]{1,0:T(8,128)(2,1)S(1)} %shard_map.61), channel_id=1, source_target_pairs={{0,2},{1,7},{2,0},{3,5},{4,6},{5,3},{6,4},{7,1},{8,10},{9,15},{10,... | collective-permute-start | bytes 786440 | tf_op jit(solution)/shard_map/ppermute | solution.py:32
  50.4 12.0 %collective-permute-start.13 = (bf16[32,4096]{1,0:T(8,128)(2,1)S(1)}, bf16[32,4096]{1,0:T(8,128)(2,1)S(1)}, u32[]{:S(2)}, u32[]{:S(2)}) collective-permute-start(bf16[32,4096]{1,0:T(8,128)(2,1)S(1)} %collective-permute-done.9.refs_2_), channel_id=1, source_target_pairs={{0,2},{1,7},{2,0},{3,5},{4,6},{5,3},{6,4},{7,1},{8,10},{9,15},{10,... | collective-permute-start | bytes 786440 | tf_op jit(solution)/shard_map/ppermute | solution.py:32
  50.5 12.5 %collective-permute-start.8 = (bf16[32,4096]{1,0:T(8,128)(2,1)S(1)}, bf16[32,4096]{1,0:T(8,128)(2,1)S(1)}, u32[]{:S(2)}, u32[]{:S(2)}) collective-permute-start(bf16[32,4096]{1,0:T(8,128)(2,1)S(1)} %shard_map.59.refs_0_), channel_id=1, source_target_pairs={{0,1},{1,0},{2,3},{3,2},{4,5},{5,4},{6,7},{7,6},{8,9},{9,8},{10,11... | collective-permute-start | bytes 786440 | tf_op jit(solution)/shard_map/ppermute | solution.py:32
  52.8 10.2 %collective-permute-start.10 = (bf16[32,4096]{1,0:T(8,128)(2,1)S(1)}, bf16[32,4096]{1,0:T(8,128)(2,1)S(1)}, u32[]{:S(2)}, u32[]{:S(2)}) collective-permute-start(bf16[32,4096]{1,0:T(8,128)(2,1)S(1)} %collective-permute-done.9.refs_2_), channel_id=1, source_target_pairs={{0,1},{1,0},{2,3},{3,2},{4,5},{5,4},{6,7},{7,6},{8,9},{9,8},{10,11... | collective-permute-start | bytes 786440 | tf_op jit(solution)/shard_map/ppermute | solution.py:32
  59.6 3.4 %collective-permute-start.12 = (bf16[32,4096]{1,0:T(8,128)(2,1)S(1)}, bf16[32,4096]{1,0:T(8,128)(2,1)S(1)}, u32[]{:S(2)}, u32[]{:S(2)}) collective-permute-start(bf16[32,4096]{1,0:T(8,128)(2,1)S(1)} %collective-permute-done.11.refs_4_), channel_id=1, source_target_pairs={{0,1},{1,0},{2,3},{3,2},{4,5},{5,4},{6,7},{7,6},{8,9},{9,8},{10,11... | collective-permute-start | bytes 786440 | tf_op jit(solution)/shard_map/ppermute | solution.py:32
  62.4 1.7 %collective-permute-start.14 = (bf16[32,4096]{1,0:T(8,128)(2,1)S(1)}, bf16[32,4096]{1,0:T(8,128)(2,1)S(1)}, u32[]{:S(2)}, u32[]{:S(2)}) collective-permute-start(bf16[32,4096]{1,0:T(8,128)(2,1)S(1)} %collective-permute-done.13.refs_6_), channel_id=1, source_target_pairs={{0,1},{1,0},{2,3},{3,2},{4,5},{5,4},{6,7},{7,6},{8,9},{9,8},{10,11... | collective-permute-start | bytes 786440 | tf_op jit(solution)/shard_map/ppermute | solution.py:32

commit v4 on v3

--- a/solution.py
+++ b/solution.py
@@ -12,7 +12,6 @@
 NORM_EPS = 1e-05
 CHIPS = 4
 CORES = 2
-FOLD = 16
 
 
 def partner(step, chip, core):
@@ -58,18 +57,22 @@
     )(*terms, *earlier)
 
 
+def normed_kernel(here, last, gain_ref, out_ref):
+    stream = total(here[...], last[...]).astype(jnp.bfloat16).astype(jnp.float32)
+    mean_sq = jnp.mean(stream * stream, axis=-1, keepdims=True)
+    out_ref[...] = (stream * lax.rsqrt(mean_sq + NORM_EPS) * gain_ref[...]).astype(jnp.bfloat16)
+
+
 def rope(x, cosine, sine):
     return x * cosine + pltpu.roll(x, x.shape[-1] // 2, 1) * sine
 
 
-def weights_kernel(wq_in, wkv_in, gain_ref, *refs):
-    wq_out, wkv_out = refs[-2:]
-    gain = gain_ref[...]
-    for source, target in ((wq_in, wq_out), (wkv_in, wkv_out)):
-        target[...] = (source[...].reshape(target.shape).astype(jnp.float32) * gain).astype(jnp.bfloat16)
-
-
-def fold_weights(w_query, w_keyval, gain, *earlier):
+def weights_kernel(wq_in, wkv_in, earlier_ref, wq_out, wkv_out):
+    wq_out[...] = wq_in[...].reshape(wq_out.shape)
+    wkv_out[...] = wkv_in[...].reshape(wkv_out.shape)
+
+
+def lay_out_weights(w_query, w_keyval, earlier):
     width, group, head_dim = w_query.shape
     depth = 512
     return pl.pallas_call(
@@ -78,9 +81,8 @@
         in_specs=[
             pl.BlockSpec((depth, group, head_dim), lambda i: (i, 0, 0)),
             pl.BlockSpec((depth, 2, head_dim), lambda i: (i, 0, 0)),
-            pl.BlockSpec((depth, 1), lambda i: (i, 0)),
-        ]
-        + [ANYWHERE] * len(earlier),
+            ANYWHERE,
+        ],
         out_specs=[
             pl.BlockSpec((depth, group * head_dim), lambda i: (i, 0)),
             pl.BlockSpec((depth, 2 * head_dim), lambda i: (i, 0)),
@@ -89,9 +91,9 @@
             pltpu.VMEM((width, group * head_dim), jnp.bfloat16),
             pltpu.VMEM((width, 2 * head_dim), jnp.bfloat16),
         ],
-        compiler_params=pltpu.CompilerParams(vmem_limit_bytes=FOLD * 2**20),
+        compiler_params=pltpu.CompilerParams(vmem_limit_bytes=16 * 2**20),
         cost_estimate=pl.CostEstimate(flops=0, bytes_accessed=20 * 2**20, transcendentals=0),
-    )(w_query, w_keyval, gain, *earlier)
+    )(w_query, w_keyval, earlier)
 
 
 def attend_kernel(place_ref, *refs):
@@ -106,15 +108,13 @@
         start = (at * CORES + (core ^ (index % CORES))) * per
         rows[pl.ds(pl.multiple_of(start, per), per), :] = piece[...]
     x = rows[...]
-    squares = jnp.sum(jnp.square(x.astype(jnp.float32)), axis=-1, keepdims=True)
-    scale = lax.rsqrt(squares * (1.0 / width) + NORM_EPS)
-    kv = jnp.dot(x, wkv_ref[...], preferred_element_type=jnp.float32) * scale
+    kv = jnp.dot(x, wkv_ref[...], preferred_element_type=jnp.float32)
     keys = rope(kv[:, :head_dim], cosk[...], sink[...]).astype(jnp.bfloat16)
     ones = jnp.ones((tokens, head_dim), jnp.bfloat16)
     values = jnp.concatenate([kv[:, head_dim:].astype(jnp.bfloat16), ones], axis=1)
     for pair in range(group // 2):
         cols = slice(pair * 2 * head_dim, (pair + 1) * 2 * head_dim)
-        q = jnp.dot(x, wq_ref[:, cols], preferred_element_type=jnp.float32) * scale
+        q = jnp.dot(x, wq_ref[:, cols], preferred_element_type=jnp.float32)
         for h in range(2):
             turned = rope(q[:, h * head_dim:(h + 1) * head_dim], cosq[...], sinq[...])
             queries[pl.ds((2 * pair + h) * tokens, tokens), :] = turned.astype(jnp.bfloat16)
@@ -159,7 +159,13 @@
     near = send(sum_after((one_mine, one_in)), step=0)
     last = send(sum_after((two_mine, two_in, far)), step=1, sections=(1, 1))
     here = send(sum_after((here_mine, here_in, near, residual[0])), sections=(1, 1))
-    made = sum_after((here, last))
+    made = pl.pallas_call(
+        normed_kernel,
+        in_specs=[IN_VMEM] * 3,
+        out_specs=IN_VMEM,
+        out_shape=jax.ShapeDtypeStruct(here.shape, jnp.bfloat16),
+        compiler_params=pltpu.CompilerParams(vmem_limit_bytes=4 * 2**20),
+    )(here, last, norm_gain)
 
     half = head_dim // 2
     frequency = ROPE_BASE ** (-jnp.arange(half, dtype=jnp.float32) * 2.0 / head_dim)
@@ -170,7 +176,7 @@
     tables = (cosine * fold, sine * fold, cosine, sine)
 
     own2 = send(made, step=1)
-    wq, wkv = fold_weights(w_query[0, :, 0], w_keyval[0, :, 0], norm_gain.reshape(width, 1), made)
+    wq, wkv = lay_out_weights(w_query[0, :, 0], w_keyval[0, :, 0], made)
     own1 = send(sum_after((made,), wq, wkv, *tables), step=0)
     own0 = made
     own3 = send(own2, step=0)

time: 70.2 us -> 68.6 us (0.977)
  starting transfers between devices: 25.4 us -> 28.6 us
  local copies, waits for them, and re-layouts: 5.68 us -> 3.42 us
  Pallas kernels: 9.05 us -> 7.44 us
    ppermute x13, starting transfers between devices: 18.3 us -> 21.4 us  [send(): return lax.ppermute(value, 'tp', [pair[:2] for pair in pairs])]
    ppermute x13, waiting for transfers between devices: 14.2 us -> 12.2 us  [send(): return lax.ppermute(value, 'tp', [pair[:2] for pair in pairs])]
    unnamed x8, local copies, waits for them, and re-layouts: 3.4 us -> 1.6 us
    pallas_call x1 -> x2, Pallas kernels: 2.74 us -> 1.21 us  [the longest x1 1 us: lay_out_weights(): pl.pallas_call(weights_kernel, grid=(width // depth,), in_specs=[pl.Block...]
    ppermute x2, waiting for transfers between devices: 14.7 us -> 16 us  [send(): return lax.ppermute(value, ('segment', 'tp'), both)]
  transfers between devices with their start and end apart: 15 -> 15, of which waited for: 8 -> 8; matrix products, arithmetic and copies ran while one was open for 2% -> 1% of each run, Pallas kernels for 5% -> 2%
where the time goes in v4:
time: 68.6 us; the launch traced here: 68.5 us
  starting transfers between devices  28.6 us (42%)
  waiting for transfers between devices  28.2 us (41%)
  Pallas kernels  7.44 us (11%)
  local copies, waits for them, and re-layouts  3.42 us (5%)
  other arithmetic  0.76 us (1%)
    ppermute x13, starting transfers between devices, send(): return lax.ppermute(value, 'tp', [pair[:2] for pair in pairs])  21.4 us
    ppermute x2, waiting for transfers between devices, send(): return lax.ppermute(value, ('segment', 'tp'), both)  16 us
    ppermute x13, waiting for transfers between devices, send(): return lax.ppermute(value, 'tp', [pair[:2] for pair in pairs])  12.2 us
    ppermute x2, starting transfers between devices, send(): return lax.ppermute(value, ('segment', 'tp'), both)  7.19 us
    pallas_call x1, Pallas kernels, per_device(): pl.pallas_call(attend_kernel, in_specs=[IN_SMEM] + [IN_VMEM] * len(operan...  5.84 us
    squeeze x1, local copies, waits for them, and re-layouts, block(): lax.dynamic_slice(blocks, (at_chip, at_core, 0, 0), (1, 1) + blocks.shape...  1.83 us
    unnamed x8, local copies, waits for them, and re-layouts  1.6 us
  transfers between devices with their start and end apart: 15, of which 8 were waited for; matrix products, arithmetic and copies ran while one was open for 1% of the time, Pallas kernels for 2%

profile of v4, /device:TPU:1, one launch (start us, length us, event | category | flops | bytes accessed | tf_op | source)
XLA Modules:
  0.0 68.5 jit_solution(1105533974996053235)
XLA Ops:
  0.0 0.0 copy-start.2
  0.0 0.0 copy-start.3
  0.0 1.8 %dynamic-slice_bitcast_fusion = (bf16[32,4096]{1,0:T(8,128)(2,1)S(1)}, bf16[32,4096]{1,0:T(8,128)(2,1)S(1)}, bf16[32,4096]{1,0:T(8,128)(2,1)S(1)}, bf16[32,4096]...) fusion(bf16[4,2,32,4096]{3,2,1,0:T(8,128)(2,1)} %bitcast.30, ...), kind=kLoop, calls=%fused_computation | loop fusion | bytes 4194328 | tf_op jit(solution)/shard_map/squeeze | solution.py:151
  1.8 3.3 %collective-permute-start.5 = (bf16[32,4096]{1,0:T(8,128)(2,1)S(1)}, bf16[32,4096]{1,0:T(8,128)(2,1)S(1)}, u32[]{:S(2)}, u32[]{:S(2)}) collective-permute-start(bf16[32,4096]{1,0:T(8,128)(2,1)S(1)} %get-tuple-element.11), channel_id=1, source_target_pairs={{0,1},{1,0},{2,3},{3,2},{4,5},{5,4},{6,7},{7,6},{8,9},{9,8},{10,11... | collective-permute-start | bytes 786440 | tf_op jit(solution)/shard_map/ppermute | solution.py:31
  5.2 0.1 collective-permute-start.1
  5.3 0.4 collective-permute-start.4
  5.7 0.7 collective-permute-done.5.refs_1_
  6.3 0.1 shard_map.57
  6.4 4.4 %collective-permute-start.6 = (bf16[32,4096]{1,0:T(8,128)(2,1)S(1)}, bf16[32,4096]{1,0:T(8,128)(2,1)S(1)}, u32[]{:S(2)}, u32[]{:S(2)}) collective-permute-start(bf16[32,4096]{1,0:T(8,128)(2,1)S(1)} %shard_map.57), channel_id=1, source_target_pairs={{0,2},{1,7},{2,0},{3,5},{4,6},{5,3},{6,4},{7,1},{8,10},{9,15},{10,... | collective-permute-start | bytes 786440 | tf_op jit(solution)/shard_map/ppermute | solution.py:31
  10.8 0.0 collective-permute-start
  10.8 0.0 collective-permute-done.1.refs_1_
  10.8 0.1 shard_map.55
  10.9 1.9 %collective-permute-start.2 = (bf16[32,4096]{1,0:T(8,128)(2,1)S(1)}, bf16[32,4096]{1,0:T(8,128)(2,1)S(1)}, u32[]{:S(2)}, u32[]{:S(2)}) collective-permute-start(bf16[32,4096]{1,0:T(8,128)(2,1)S(1)} %shard_map.55), channel_id=1, source_target_pairs={{0,2},{1,7},{2,0},{3,5},{4,6},{5,3},{6,4},{7,1},{8,10},{9,15},{10,... | collective-permute-start | bytes 786440 | tf_op jit(solution)/shard_map/ppermute | solution.py:31
  12.8 0.0 collective-permute-done.4.refs_1_
  12.8 2.5 %collective-permute-done.6.refs_2_ = bf16[32,4096]{1,0:T(8,128)(2,1)S(1)} collective-permute-done((bf16[32,4096]{1,0:T(8,128)(2,1)S(1)}, bf16[32,4096]{1,0:T(8,128)(2,1)S(1)}, u32[]{:S(2)}, u32[]{:S(2)}) %collective-permute-start.6) | collective-permute-done | bytes 262176 | tf_op jit(solution)/shard_map/ppermute | solution.py:31
  15.2 0.1 shard_map.58
  15.4 5.7 %collective-permute-start.7 = (bf16[32,4096]{1,0:T(8,128)(2,1)S(1)}, bf16[32,4096]{1,0:T(8,128)(2,1)S(1)}, u32[]{:S(2)}, u32[]{:S(2)}) collective-permute-start(bf16[32,4096]{1,0:T(8,128)(2,1)S(1)} %shard_map.58), channel_id=1, source_target_pairs={{0,14},{1,11},{2,12},{3,9},{4,10},{5,15},{6,8},{7,13},{8,22},{9,19... | collective-permute-start | bytes 786440 | tf_op jit(solution)/shard_map/ppermute | solution.py:33
  21.1 0.0 collective-permute-done.refs_1_
  21.1 0.8 %collective-permute-done.2.refs_2_ = bf16[32,4096]{1,0:T(8,128)(2,1)S(1)} collective-permute-done((bf16[32,4096]{1,0:T(8,128)(2,1)S(1)}, bf16[32,4096]{1,0:T(8,128)(2,1)S(1)}, u32[]{:S(2)}, u32[]{:S(2)}) %collective-permute-start.2) | collective-permute-done | bytes 262176 | tf_op jit(solution)/shard_map/ppermute | solution.py:31
  21.9 0.0 copy-done.2
  21.9 0.1 shard_map.56
  22.1 1.4 %collective-permute-start.3 = (bf16[32,4096]{1,0:T(8,128)(2,1)S(1)}, bf16[32,4096]{1,0:T(8,128)(2,1)S(1)}, u32[]{:S(2)}, u32[]{:S(2)}) collective-permute-start(bf16[32,4096]{1,0:T(8,128)(2,1)S(1)} %shard_map.56), channel_id=1, source_target_pairs={{0,8},{1,9},{2,10},{3,11},{4,12},{5,13},{6,14},{7,15},{8,16},{9,17... | collective-permute-start | bytes 786440 | tf_op jit(solution)/shard_map/ppermute | solution.py:33
  23.5 11.2 %collective-permute-done.7.last = bf16[32,4096]{1,0:T(8,128)(2,1)S(1)} collective-permute-done((bf16[32,4096]{1,0:T(8,128)(2,1)S(1)}, bf16[32,4096]{1,0:T(8,128)(2,1)S(1)}, u32[]{:S(2)}, u32[]{:S(2)}) %collective-permute-start.7) | collective-permute-done | bytes 262176 | tf_op jit(solution)/shard_map/ppermute | solution.py:33
  34.7 4.8 %collective-permute-done.3.here = bf16[32,4096]{1,0:T(8,128)(2,1)S(1)} collective-permute-done((bf16[32,4096]{1,0:T(8,128)(2,1)S(1)}, bf16[32,4096]{1,0:T(8,128)(2,1)S(1)}, u32[]{:S(2)}, u32[]{:S(2)}) %collective-permute-start.3) | collective-permute-done | bytes 262176 | tf_op jit(solution)/shard_map/ppermute | solution.py:33
  39.5 0.0 copy-done.3
  39.5 0.2 shard_map.59.earlier_ref.refs_0_
  39.7 0.1 collective-permute-start.9
  39.8 0.5 fusion
  40.4 0.1 pad_maximum_fusion
  40.5 0.0 copy-done
  40.5 0.0 copy-start.1
  40.5 1.6 %copy-done.1 = bf16[1,4096,1,2,128]{4,3,2,1,0:T(2,128)(2,1)S(1)} copy-done((bf16[1,4096,1,2,128]{4,3,2,1,0:T(2,128)(2,1)S(1)}, bf16[1,4096,1,2,128]{4,3,2,1,0:T(2,128)(2,1)}, u32[]{:S(2)}) %copy-start.1) | copy-done | bytes 2097176
  42.1 1.0 %shard_map.60 = (bf16[4096,1024]{1,0:T(8,128)(2,1)S(1)}, bf16[4096,256]{1,0:T(8,128)(2,1)S(1)}) custom-call(bf16[4096,8,128]{2,1,0:T(8,128)(2,1)S(1)} %bitcast.27, bf16[4096,2,128]{2,1,0:T(2,128)(2,1)S(1)} %bitcast.28, bf16[32,4096]{1,0:T(8,128)(2,1)S(1)} %shard_map.59.earlier_ref.refs_0_), custom_call_target="tpu_custom_call" | custom-call | bytes 20971520 | tf_op jit(solution)/shard_map/pallas_call | solution.py:78
  43.2 4.7 %collective-permute-start.11 = (bf16[32,4096]{1,0:T(8,128)(2,1)S(1)}, bf16[32,4096]{1,0:T(8,128)(2,1)S(1)}, u32[]{:S(2)}, u32[]{:S(2)}) collective-permute-start(bf16[32,4096]{1,0:T(8,128)(2,1)S(1)} %shard_map.61), channel_id=1, source_target_pairs={{0,2},{1,7},{2,0},{3,5},{4,6},{5,3},{6,4},{7,1},{8,10},{9,15},{10,... | collective-permute-start | bytes 786440 | tf_op jit(solution)/shard_map/ppermute | solution.py:31
  47.8 0.0 collective-permute-done.9.refs_2_
  47.8 3.0 %collective-permute-start.13 = (bf16[32,4096]{1,0:T(8,128)(2,1)S(1)}, bf16[32,4096]{1,0:T(8,128)(2,1)S(1)}, u32[]{:S(2)}, u32[]{:S(2)}) collective-permute-start(bf16[32,4096]{1,0:T(8,128)(2,1)S(1)} %collective-permute-done.9.refs_2_), channel_id=1, source_target_pairs={{0,2},{1,7},{2,0},{3,5},{4,6},{5,3},{6,4},{7,1},{8,10},{9,15},{10,... | collective-permute-start | bytes 786440 | tf_op jit(solution)/shard_map/ppermute | solution.py:31
  50.8 0.5 collective-permute-start.8
  51.3 0.0 collective-permute-start.10
  51.3 4.1 %collective-permute-done.11.refs_4_ = bf16[32,4096]{1,0:T(8,128)(2,1)S(1)} collective-permute-done((bf16[32,4096]{1,0:T(8,128)(2,1)S(1)}, bf16[32,4096]{1,0:T(8,128)(2,1)S(1)}, u32[]{:S(2)}, u32[]{:S(2)}) %collective-permute-start.11) | collective-permute-done | bytes 262176 | tf_op jit(solution)/shard_map/ppermute | solution.py:31
  55.5 1.0 %collective-permute-start.12 = (bf16[32,4096]{1,0:T(8,128)(2,1)S(1)}, bf16[32,4096]{1,0:T(8,128)(2,1)S(1)}, u32[]{:S(2)}, u32[]{:S(2)}) collective-permute-start(bf16[32,4096]{1,0:T(8,128)(2,1)S(1)} %collective-permute-done.11.refs_4_), channel_id=1, source_target_pairs={{0,1},{1,0},{2,3},{3,2},{4,5},{5,4},{6,7},{7,6},{8,9},{9,8},{10,11... | collective-permute-start | bytes 786440 | tf_op jit(solution)/shard_map/ppermute | solution.py:31
  56.5 3.0 %collective-permute-done.13.refs_6_ = bf16[32,4096]{1,0:T(8,128)(2,1)S(1)} collective-permute-done((bf16[32,4096]{1,0:T(8,128)(2,1)S(1)}, bf16[32,4096]{1,0:T(8,128)(2,1)S(1)}, u32[]{:S(2)}, u32[]{:S(2)}) %collective-permute-start.13) | collective-permute-done | bytes 262176 | tf_op jit(solution)/shard_map/ppermute | solution.py:31
  59.5 2.0 %collective-permute-start.14 = (bf16[32,4096]{1,0:T(8,128)(2,1)S(1)}, bf16[32,4096]{1,0:T(8,128)(2,1)S(1)}, u32[]{:S(2)}, u32[]{:S(2)}) collective-permute-start(bf16[32,4096]{1,0:T(8,128)(2,1)S(1)} %collective-permute-done.13.refs_6_), channel_id=1, source_target_pairs={{0,1},{1,0},{2,3},{3,2},{4,5},{5,4},{6,7},{7,6},{8,9},{9,8},{10,11... | collective-permute-start | bytes 786440 | tf_op jit(solution)/shard_map/ppermute | solution.py:31
  61.5 0.1 pad_add_fusion.place_ref
  61.6 0.0 collective-permute-done.8.refs_1_
  61.6 0.0 collective-permute-done.10.refs_3_
  61.6 0.0 collective-permute-done.12.refs_5_
  61.6 1.1 %collective-permute-done.14.refs_7_ = bf16[32,4096]{1,0:T(8,128)(2,1)S(1)} collective-permute-done((bf16[32,4096]{1,0:T(8,128)(2,1)S(1)}, bf16[32,4096]{1,0:T(8,128)(2,1)S(1)}, u32[]{:S(2)}, u32[]{:S(2)}) %collective-permute-start.14) | collective-permute-done | bytes 262176 | tf_op jit(solution)/shard_map/ppermute | solution.py:31
  62.7 5.8 %shard_map.62 = bf16[256,8,128]{2,1,0:T(8,128)(2,1)} custom-call(s32[4]{0:T(128)S(1)} %pad_add_fusion.place_ref, bf16[32,4096]{1,0:T(8,128)(2,1)S(1)} %shard_map.59.earlier_ref.refs_0_, bf16[32,4096]{1,0:T(8,128)(2,1)S(1)} %collective-permute-done.8.refs_1_, bf16[32,4096]{1,0:T(8,128)(2,1)S(1)} %collective-permute-done.9.refs_2_, ...), custom_call_target="tpu_custom_call" | custom-call | flops 2684354560 | bytes 14680064 | tf_op jit(solution)/shard_map/pallas_call | solution.py:188
  (4 shorter events, 0.0 us)
Async XLA Ops:
  0.0 21.9 %copy-start.2 = (bf16[1,32,4096]{2,1,0:T(8,128)(2,1)S(1)}, bf16[1,32,4096]{2,1,0:T(8,128)(2,1)}, u32[]{:S(2)}) copy-start(bf16[1,32,4096]{2,1,0:T(8,128)(2,1)} %param.6) | copy-start | bytes 786436
  0.0 39.5 %copy-start.3 = (f32[1,4096]{1,0:T(1,128)S(1)}, f32[1,4096]{1,0:T(1,128)}, u32[]{:S(2)}) copy-start(f32[1,4096]{1,0:T(1,128)} %gain_ref.1) | copy-start | bytes 49156
  0.0 40.5 %copy-start = (bf16[1,4096,1,8,128]{4,3,2,1,0:T(8,128)(2,1)S(1)}, bf16[1,4096,1,8,128]{4,3,2,1,0:T(8,128)(2,1)}, u32[]{:S(2)}) copy-start(bf16[1,4096,1,8,128]{4,3,2,1,0:T(8,128)(2,1)} %param.8) | copy-start | bytes 25165828
  1.8 4.5 %collective-permute-start.5 = (bf16[32,4096]{1,0:T(8,128)(2,1)S(1)}, bf16[32,4096]{1,0:T(8,128)(2,1)S(1)}, u32[]{:S(2)}, u32[]{:S(2)}) collective-permute-start(bf16[32,4096]{1,0:T(8,128)(2,1)S(1)} %get-tuple-element.11), channel_id=1, source_target_pairs={{0,1},{1,0},{2,3},{3,2},{4,5},{5,4},{6,7},{7,6},{8,9},{9,8},{10,11... | collective-permute-start | bytes 786440 | tf_op jit(solution)/shard_map/ppermute | solution.py:31
  5.2 5.6 %collective-permute-start.1 = (bf16[32,4096]{1,0:T(8,128)(2,1)S(1)}, bf16[32,4096]{1,0:T(8,128)(2,1)S(1)}, u32[]{:S(2)}, u32[]{:S(2)}) collective-permute-start(bf16[32,4096]{1,0:T(8,128)(2,1)S(1)} %get-tuple-element.15), channel_id=1, source_target_pairs={{0,1},{1,0},{2,3},{3,2},{4,5},{5,4},{6,7},{7,6},{8,9},{9,8},{10,11... | collective-permute-start | bytes 786440 | tf_op jit(solution)/shard_map/ppermute | solution.py:31
  5.3 7.5 %collective-permute-start.4 = (bf16[32,4096]{1,0:T(8,128)(2,1)S(1)}, bf16[32,4096]{1,0:T(8,128)(2,1)S(1)}, u32[]{:S(2)}, u32[]{:S(2)}) collective-permute-start(bf16[32,4096]{1,0:T(8,128)(2,1)S(1)} %get-tuple-element.13), channel_id=1, source_target_pairs={{0,1},{1,0},{2,3},{3,2},{4,5},{5,4},{6,7},{7,6},{8,9},{9,8},{10,11... | collective-permute-start | bytes 786440 | tf_op jit(solution)/shard_map/ppermute | solution.py:31
  6.4 8.9 %collective-permute-start.6 = (bf16[32,4096]{1,0:T(8,128)(2,1)S(1)}, bf16[32,4096]{1,0:T(8,128)(2,1)S(1)}, u32[]{:S(2)}, u32[]{:S(2)}) collective-permute-start(bf16[32,4096]{1,0:T(8,128)(2,1)S(1)} %shard_map.57), channel_id=1, source_target_pairs={{0,2},{1,7},{2,0},{3,5},{4,6},{5,3},{6,4},{7,1},{8,10},{9,15},{10,... | collective-permute-start | bytes 786440 | tf_op jit(solution)/shard_map/ppermute | solution.py:31
  10.8 10.3 %collective-permute-start = (bf16[32,4096]{1,0:T(8,128)(2,1)S(1)}, bf16[32,4096]{1,0:T(8,128)(2,1)S(1)}, u32[]{:S(2)}, u32[]{:S(2)}) collective-permute-start(bf16[32,4096]{1,0:T(8,128)(2,1)S(1)} %get-tuple-element.17), channel_id=1, source_target_pairs={{0,1},{1,0},{2,3},{3,2},{4,5},{5,4},{6,7},{7,6},{8,9},{9,8},{10,11... | collective-permute-start | bytes 786440 | tf_op jit(solution)/shard_map/ppermute | solution.py:31
  10.9 11.1 %collective-permute-start.2 = (bf16[32,4096]{1,0:T(8,128)(2,1)S(1)}, bf16[32,4096]{1,0:T(8,128)(2,1)S(1)}, u32[]{:S(2)}, u32[]{:S(2)}) collective-permute-start(bf16[32,4096]{1,0:T(8,128)(2,1)S(1)} %shard_map.55), channel_id=1, source_target_pairs={{0,2},{1,7},{2,0},{3,5},{4,6},{5,3},{6,4},{7,1},{8,10},{9,15},{10,... | collective-permute-start | bytes 786440 | tf_op jit(solution)/shard_map/ppermute | solution.py:31
  15.4 19.4 %collective-permute-start.7 = (bf16[32,4096]{1,0:T(8,128)(2,1)S(1)}, bf16[32,4096]{1,0:T(8,128)(2,1)S(1)}, u32[]{:S(2)}, u32[]{:S(2)}) collective-permute-start(bf16[32,4096]{1,0:T(8,128)(2,1)S(1)} %shard_map.58), channel_id=1, source_target_pairs={{0,14},{1,11},{2,12},{3,9},{4,10},{5,15},{6,8},{7,13},{8,22},{9,19... | collective-permute-start | bytes 786440 | tf_op jit(solution)/shard_map/ppermute | solution.py:33
  22.1 17.5 %collective-permute-start.3 = (bf16[32,4096]{1,0:T(8,128)(2,1)S(1)}, bf16[32,4096]{1,0:T(8,128)(2,1)S(1)}, u32[]{:S(2)}, u32[]{:S(2)}) collective-permute-start(bf16[32,4096]{1,0:T(8,128)(2,1)S(1)} %shard_map.56), channel_id=1, source_target_pairs={{0,8},{1,9},{2,10},{3,11},{4,12},{5,13},{6,14},{7,15},{8,16},{9,17... | collective-permute-start | bytes 786440 | tf_op jit(solution)/shard_map/ppermute | solution.py:33
  39.7 8.1 %collective-permute-start.9 = (bf16[32,4096]{1,0:T(8,128)(2,1)S(1)}, bf16[32,4096]{1,0:T(8,128)(2,1)S(1)}, u32[]{:S(2)}, u32[]{:S(2)}) collective-permute-start(bf16[32,4096]{1,0:T(8,128)(2,1)S(1)} %shard_map.59.earlier_ref.refs_0_), channel_id=1, source_target_pairs={{0,6},{1,3},{2,4},{3,1},{4,2},{5,7},{6,0},{7,5},{8,14},{9,11},{10,... | collective-permute-start | bytes 786440 | tf_op jit(solution)/shard_map/ppermute | solution.py:31
  40.5 1.6 %copy-start.1 = (bf16[1,4096,1,2,128]{4,3,2,1,0:T(2,128)(2,1)S(1)}, bf16[1,4096,1,2,128]{4,3,2,1,0:T(2,128)(2,1)}, u32[]{:S(2)}) copy-start(bf16[1,4096,1,2,128]{4,3,2,1,0:T(2,128)(2,1)} %param.9) | copy-start | bytes 6291460
  43.2 12.3 %collective-permute-start.11 = (bf16[32,4096]{1,0:T(8,128)(2,1)S(1)}, bf16[32,4096]{1,0:T(8,128)(2,1)S(1)}, u32[]{:S(2)}, u32[]{:S(2)}) collective-permute-start(bf16[32,4096]{1,0:T(8,128)(2,1)S(1)} %shard_map.61), channel_id=1, source_target_pairs={{0,2},{1,7},{2,0},{3,5},{4,6},{5,3},{6,4},{7,1},{8,10},{9,15},{10,... | collective-permute-start | bytes 786440 | tf_op jit(solution)/shard_map/ppermute | solution.py:31
  47.8 11.7 %collective-permute-start.13 = (bf16[32,4096]{1,0:T(8,128)(2,1)S(1)}, bf16[32,4096]{1,0:T(8,128)(2,1)S(1)}, u32[]{:S(2)}, u32[]{:S(2)}) collective-permute-start(bf16[32,4096]{1,0:T(8,128)(2,1)S(1)} %collective-permute-done.9.refs_2_), channel_id=1, source_target_pairs={{0,2},{1,7},{2,0},{3,5},{4,6},{5,3},{6,4},{7,1},{8,10},{9,15},{10,... | collective-permute-start | bytes 786440 | tf_op jit(solution)/shard_map/ppermute | solution.py:31
  50.8 10.7 %collective-permute-start.8 = (bf16[32,4096]{1,0:T(8,128)(2,1)S(1)}, bf16[32,4096]{1,0:T(8,128)(2,1)S(1)}, u32[]{:S(2)}, u32[]{:S(2)}) collective-permute-start(bf16[32,4096]{1,0:T(8,128)(2,1)S(1)} %shard_map.59.earlier_ref.refs_0_), channel_id=1, source_target_pairs={{0,1},{1,0},{2,3},{3,2},{4,5},{5,4},{6,7},{7,6},{8,9},{9,8},{10,11... | collective-permute-start | bytes 786440 | tf_op jit(solution)/shard_map/ppermute | solution.py:31
  51.3 10.2 %collective-permute-start.10 = (bf16[32,4096]{1,0:T(8,128)(2,1)S(1)}, bf16[32,4096]{1,0:T(8,128)(2,1)S(1)}, u32[]{:S(2)}, u32[]{:S(2)}) collective-permute-start(bf16[32,4096]{1,0:T(8,128)(2,1)S(1)} %collective-permute-done.9.refs_2_), channel_id=1, source_target_pairs={{0,1},{1,0},{2,3},{3,2},{4,5},{5,4},{6,7},{7,6},{8,9},{9,8},{10,11... | collective-permute-start | bytes 786440 | tf_op jit(solution)/shard_map/ppermute | solution.py:31
  55.5 6.1 %collective-permute-start.12 = (bf16[32,4096]{1,0:T(8,128)(2,1)S(1)}, bf16[32,4096]{1,0:T(8,128)(2,1)S(1)}, u32[]{:S(2)}, u32[]{:S(2)}) collective-permute-start(bf16[32,4096]{1,0:T(8,128)(2,1)S(1)} %collective-permute-done.11.refs_4_), channel_id=1, source_target_pairs={{0,1},{1,0},{2,3},{3,2},{4,5},{5,4},{6,7},{7,6},{8,9},{9,8},{10,11... | collective-permute-start | bytes 786440 | tf_op jit(solution)/shard_map/ppermute | solution.py:31
  59.5 3.2 %collective-permute-start.14 = (bf16[32,4096]{1,0:T(8,128)(2,1)S(1)}, bf16[32,4096]{1,0:T(8,128)(2,1)S(1)}, u32[]{:S(2)}, u32[]{:S(2)}) collective-permute-start(bf16[32,4096]{1,0:T(8,128)(2,1)S(1)} %collective-permute-done.13.refs_6_), channel_id=1, source_target_pairs={{0,1},{1,0},{2,3},{3,2},{4,5},{5,4},{6,7},{7,6},{8,9},{9,8},{10,11... | collective-permute-start | bytes 786440 | tf_op jit(solution)/shard_map/ppermute | solution.py:31

commit v5 on v4

--- a/solution.py
+++ b/solution.py
@@ -57,10 +57,10 @@
     )(*terms, *earlier)
 
 
-def normed_kernel(here, last, gain_ref, out_ref):
+def normed_kernel(here, last, gain_ref, *refs):
     stream = total(here[...], last[...]).astype(jnp.bfloat16).astype(jnp.float32)
     mean_sq = jnp.mean(stream * stream, axis=-1, keepdims=True)
-    out_ref[...] = (stream * lax.rsqrt(mean_sq + NORM_EPS) * gain_ref[...]).astype(jnp.bfloat16)
+    refs[-1][...] = (stream * lax.rsqrt(mean_sq + NORM_EPS) * gain_ref[...]).astype(jnp.bfloat16)
 
 
 def rope(x, cosine, sine):
@@ -150,6 +150,14 @@
     def block(at_chip, at_core):
         return lax.dynamic_slice(blocks, (at_chip, at_core, 0, 0), (1, 1) + blocks.shape[2:])[0, 0]
 
+    half = head_dim // 2
+    frequency = ROPE_BASE ** (-jnp.arange(half, dtype=jnp.float32) * 2.0 / head_dim)
+    angles = jnp.arange(tokens).astype(jnp.float32)[:, None] * frequency[None, :]
+    cosine = jnp.concatenate([jnp.cos(angles)] * 2, axis=1)
+    sine = jnp.concatenate([-jnp.sin(angles), jnp.sin(angles)], axis=1)
+    fold = math.log2(math.e) / math.sqrt(head_dim)
+    tables = (cosine * fold, sine * fold, cosine, sine)
+
     place = jnp.stack([chip, core, one, two]).astype(jnp.int32)
     far_in = send(block(chip ^ 2, 1 - core), flip=1)
     one_in, two_in, here_in = (send(block(at, 1 - core), flip=1) for at in (two, one, chip))
@@ -161,23 +169,15 @@
     here = send(sum_after((here_mine, here_in, near, residual[0])), sections=(1, 1))
     made = pl.pallas_call(
         normed_kernel,
-        in_specs=[IN_VMEM] * 3,
+        in_specs=[IN_VMEM] * 3 + [ANYWHERE] * len(tables),
         out_specs=IN_VMEM,
         out_shape=jax.ShapeDtypeStruct(here.shape, jnp.bfloat16),
         compiler_params=pltpu.CompilerParams(vmem_limit_bytes=4 * 2**20),
-    )(here, last, norm_gain)
-
-    half = head_dim // 2
-    frequency = ROPE_BASE ** (-jnp.arange(half, dtype=jnp.float32) * 2.0 / head_dim)
-    angles = jnp.arange(tokens).astype(jnp.float32)[:, None] * frequency[None, :]
-    cosine = jnp.concatenate([jnp.cos(angles)] * 2, axis=1)
-    sine = jnp.concatenate([-jnp.sin(angles), jnp.sin(angles)], axis=1)
-    fold = math.log2(math.e) / math.sqrt(head_dim)
-    tables = (cosine * fold, sine * fold, cosine, sine)
+    )(here, last, norm_gain, *tables)
 
     own2 = send(made, step=1)
     wq, wkv = lay_out_weights(w_query[0, :, 0], w_keyval[0, :, 0], made)
-    own1 = send(sum_after((made,), wq, wkv, *tables), step=0)
+    own1 = send(sum_after((made,), wq, wkv), step=0)
     own0 = made
     own3 = send(own2, step=0)
     pieces = []

time: 68.6 us -> 72.1 us (1.051)
  starting transfers between devices: 28.6 us -> 32.3 us
  local copies, waits for them, and re-layouts: 3.42 us -> 1.84 us
  waiting for transfers between devices: 28.2 us -> 29.6 us
    ppermute x13, starting transfers between devices: 21.4 us -> 25.1 us  [send(): return lax.ppermute(value, 'tp', [pair[:2] for pair in pairs])]
    ppermute x13, waiting for transfers between devices: 12.2 us -> 14.9 us  [send(): return lax.ppermute(value, 'tp', [pair[:2] for pair in pairs])]
    unnamed x8, local copies, waits for them, and re-layouts: 1.6 us -> 0.02 us
    ppermute x2, waiting for transfers between devices: 16 us -> 14.7 us  [send(): return lax.ppermute(value, ('segment', 'tp'), both)]
  transfers between devices with their start and end apart: 15 -> 15, of which waited for: 8 -> 9; matrix products, arithmetic and copies ran while one was open for 1% -> 1% of each run, Pallas kernels for 2% -> 2%
where the time goes in v5:
time: 72.1 us; the launch traced here: 72 us
  starting transfers between devices  32.3 us (45%)
  waiting for transfers between devices  29.6 us (41%)
  Pallas kernels  7.45 us (10%)
  local copies, waits for them, and re-layouts  1.84 us (3%)
  other arithmetic  0.76 us (1%)
    ppermute x13, starting transfers between devices, send(): return lax.ppermute(value, 'tp', [pair[:2] for pair in pairs])  25.1 us
    ppermute x13, waiting for transfers between devices, send(): return lax.ppermute(value, 'tp', [pair[:2] for pair in pairs])  14.9 us
    ppermute x2, waiting for transfers between devices, send(): return lax.ppermute(value, ('segment', 'tp'), both)  14.7 us
    ppermute x2, starting transfers between devices, send(): return lax.ppermute(value, ('segment', 'tp'), both)  7.17 us
    pallas_call x1, Pallas kernels, per_device(): pl.pallas_call(attend_kernel, in_specs=[IN_SMEM] + [IN_VMEM] * len(operan...  5.85 us
    squeeze x1, local copies, waits for them, and re-layouts, block(): lax.dynamic_slice(blocks, (at_chip, at_core, 0, 0), (1, 1) + blocks.shape...  1.83 us
  transfers between devices with their start and end apart: 15, of which 9 were waited for; matrix products, arithmetic and copies ran while one was open for 1% of the time, Pallas kernels for 2%

profile of v5, /device:TPU:1, one launch (start us, length us, event | category | flops | bytes accessed | tf_op | source)
XLA Modules:
  0.0 72.0 jit_solution(14945688470682968856)
XLA Ops:
  0.0 0.0 copy-start.2
  0.0 0.0 copy-start
  0.0 1.8 %dynamic-slice_bitcast_fusion = (bf16[32,4096]{1,0:T(8,128)(2,1)S(1)}, bf16[32,4096]{1,0:T(8,128)(2,1)S(1)}, bf16[32,4096]{1,0:T(8,128)(2,1)S(1)}, bf16[32,4096]...) fusion(bf16[4,2,32,4096]{3,2,1,0:T(8,128)(2,1)} %bitcast.30, ...), kind=kLoop, calls=%fused_computation | loop fusion | bytes 4194328 | tf_op jit(solution)/shard_map/squeeze | solution.py:151
  1.8 3.3 %collective-permute-start.5 = (bf16[32,4096]{1,0:T(8,128)(2,1)S(1)}, bf16[32,4096]{1,0:T(8,128)(2,1)S(1)}, u32[]{:S(2)}, u32[]{:S(2)}) collective-permute-start(bf16[32,4096]{1,0:T(8,128)(2,1)S(1)} %get-tuple-element.11), channel_id=1, source_target_pairs={{0,1},{1,0},{2,3},{3,2},{4,5},{5,4},{6,7},{7,6},{8,9},{9,8},{10,11... | collective-permute-start | bytes 786440 | tf_op jit(solution)/shard_map/ppermute | solution.py:31
  5.2 0.1 collective-permute-start.1
  5.3 0.4 collective-permute-start.4
  5.7 0.7 collective-permute-done.5.refs_1_
  6.3 0.1 shard_map.57
  6.4 4.4 %collective-permute-start.6 = (bf16[32,4096]{1,0:T(8,128)(2,1)S(1)}, bf16[32,4096]{1,0:T(8,128)(2,1)S(1)}, u32[]{:S(2)}, u32[]{:S(2)}) collective-permute-start(bf16[32,4096]{1,0:T(8,128)(2,1)S(1)} %shard_map.57), channel_id=1, source_target_pairs={{0,2},{1,7},{2,0},{3,5},{4,6},{5,3},{6,4},{7,1},{8,10},{9,15},{10,... | collective-permute-start | bytes 786440 | tf_op jit(solution)/shard_map/ppermute | solution.py:31
  10.8 0.0 collective-permute-start
  10.8 0.0 collective-permute-done.1.refs_1_
  10.8 0.1 shard_map.55
  10.9 1.9 %collective-permute-start.2 = (bf16[32,4096]{1,0:T(8,128)(2,1)S(1)}, bf16[32,4096]{1,0:T(8,128)(2,1)S(1)}, u32[]{:S(2)}, u32[]{:S(2)}) collective-permute-start(bf16[32,4096]{1,0:T(8,128)(2,1)S(1)} %shard_map.55), channel_id=1, source_target_pairs={{0,2},{1,7},{2,0},{3,5},{4,6},{5,3},{6,4},{7,1},{8,10},{9,15},{10,... | collective-permute-start | bytes 786440 | tf_op jit(solution)/shard_map/ppermute | solution.py:31
  12.8 0.0 collective-permute-done.4.refs_1_
  12.8 2.5 %collective-permute-done.6.refs_2_ = bf16[32,4096]{1,0:T(8,128)(2,1)S(1)} collective-permute-done((bf16[32,4096]{1,0:T(8,128)(2,1)S(1)}, bf16[32,4096]{1,0:T(8,128)(2,1)S(1)}, u32[]{:S(2)}, u32[]{:S(2)}) %collective-permute-start.6) | collective-permute-done | bytes 262176 | tf_op jit(solution)/shard_map/ppermute | solution.py:31
  15.2 0.1 shard_map.58
  15.3 0.0 copy-start.1
  15.4 5.7 %collective-permute-start.7 = (bf16[32,4096]{1,0:T(8,128)(2,1)S(1)}, bf16[32,4096]{1,0:T(8,128)(2,1)S(1)}, u32[]{:S(2)}, u32[]{:S(2)}) collective-permute-start(bf16[32,4096]{1,0:T(8,128)(2,1)S(1)} %shard_map.58), channel_id=1, source_target_pairs={{0,14},{1,11},{2,12},{3,9},{4,10},{5,15},{6,8},{7,13},{8,22},{9,19... | collective-permute-start | bytes 786440 | tf_op jit(solution)/shard_map/ppermute | solution.py:33
  21.1 0.0 collective-permute-done.refs_1_
  21.1 0.9 %collective-permute-done.2.refs_2_ = bf16[32,4096]{1,0:T(8,128)(2,1)S(1)} collective-permute-done((bf16[32,4096]{1,0:T(8,128)(2,1)S(1)}, bf16[32,4096]{1,0:T(8,128)(2,1)S(1)}, u32[]{:S(2)}, u32[]{:S(2)}) %collective-permute-start.2) | collective-permute-done | bytes 262176 | tf_op jit(solution)/shard_map/ppermute | solution.py:31
  21.9 0.0 copy-done.2
  21.9 0.1 shard_map.56
  22.1 1.4 %collective-permute-start.3 = (bf16[32,4096]{1,0:T(8,128)(2,1)S(1)}, bf16[32,4096]{1,0:T(8,128)(2,1)S(1)}, u32[]{:S(2)}, u32[]{:S(2)}) collective-permute-start(bf16[32,4096]{1,0:T(8,128)(2,1)S(1)} %shard_map.56), channel_id=1, source_target_pairs={{0,8},{1,9},{2,10},{3,11},{4,12},{5,13},{6,14},{7,15},{8,16},{9,17... | collective-permute-start | bytes 786440 | tf_op jit(solution)/shard_map/ppermute | solution.py:33
  23.5 0.5 fusion
  24.1 0.1 pad_maximum_fusion
  24.2 10.6 %collective-permute-done.7.last = bf16[32,4096]{1,0:T(8,128)(2,1)S(1)} collective-permute-done((bf16[32,4096]{1,0:T(8,128)(2,1)S(1)}, bf16[32,4096]{1,0:T(8,128)(2,1)S(1)}, u32[]{:S(2)}, u32[]{:S(2)}) %collective-permute-start.7) | collective-permute-done | bytes 262176 | tf_op jit(solution)/shard_map/ppermute | solution.py:33
  34.8 4.1 %collective-permute-done.3.here = bf16[32,4096]{1,0:T(8,128)(2,1)S(1)} collective-permute-done((bf16[32,4096]{1,0:T(8,128)(2,1)S(1)}, bf16[32,4096]{1,0:T(8,128)(2,1)S(1)}, u32[]{:S(2)}, u32[]{:S(2)}) %collective-permute-start.3) | collective-permute-done | bytes 262176 | tf_op jit(solution)/shard_map/ppermute | solution.py:33
  38.9 0.0 copy-done.3
  39.0 0.2 shard_map.59.earlier_ref.refs_0_
  39.2 0.6 collective-permute-start.9
  39.8 0.0 copy-done
  39.8 0.0 copy-done.1
  39.8 1.0 %shard_map.60 = (bf16[4096,1024]{1,0:T(8,128)(2,1)S(1)}, bf16[4096,256]{1,0:T(8,128)(2,1)S(1)}) custom-call(bf16[4096,8,128]{2,1,0:T(8,128)(2,1)S(1)} %bitcast.27, bf16[4096,2,128]{2,1,0:T(2,128)(2,1)S(1)} %bitcast.28, bf16[32,4096]{1,0:T(8,128)(2,1)S(1)} %shard_map.59.earlier_ref.refs_0_), custom_call_target="tpu_custom_call" | custom-call | bytes 20971520 | tf_op jit(solution)/shard_map/pallas_call | solution.py:78
  40.8 4.1 %collective-permute-start.11 = (bf16[32,4096]{1,0:T(8,128)(2,1)S(1)}, bf16[32,4096]{1,0:T(8,128)(2,1)S(1)}, u32[]{:S(2)}, u32[]{:S(2)}) collective-permute-start(bf16[32,4096]{1,0:T(8,128)(2,1)S(1)} %shard_map.61), channel_id=1, source_target_pairs={{0,2},{1,7},{2,0},{3,5},{4,6},{5,3},{6,4},{7,1},{8,10},{9,15},{10,... | collective-permute-start | bytes 786440 | tf_op jit(solution)/shard_map/ppermute | solution.py:31
  44.8 6.0 %collective-permute-done.9.refs_2_ = bf16[32,4096]{1,0:T(8,128)(2,1)S(1)} collective-permute-done((bf16[32,4096]{1,0:T(8,128)(2,1)S(1)}, bf16[32,4096]{1,0:T(8,128)(2,1)S(1)}, u32[]{:S(2)}, u32[]{:S(2)}) %collective-permute-start.9) | collective-permute-done | bytes 262176 | tf_op jit(solution)/shard_map/ppermute | solution.py:31
  50.9 0.0 collective-permute-start.13
  50.9 4.1 %collective-permute-start.8 = (bf16[32,4096]{1,0:T(8,128)(2,1)S(1)}, bf16[32,4096]{1,0:T(8,128)(2,1)S(1)}, u32[]{:S(2)}, u32[]{:S(2)}) collective-permute-start(bf16[32,4096]{1,0:T(8,128)(2,1)S(1)} %shard_map.59.earlier_ref.refs_0_), channel_id=1, source_target_pairs={{0,1},{1,0},{2,3},{3,2},{4,5},{5,4},{6,7},{7,6},{8,9},{9,8},{10,11... | collective-permute-start | bytes 786440 | tf_op jit(solution)/shard_map/ppermute | solution.py:31
  55.0 0.0 collective-permute-start.10
  55.0 1.0 %collective-permute-done.11.refs_4_ = bf16[32,4096]{1,0:T(8,128)(2,1)S(1)} collective-permute-done((bf16[32,4096]{1,0:T(8,128)(2,1)S(1)}, bf16[32,4096]{1,0:T(8,128)(2,1)S(1)}, u32[]{:S(2)}, u32[]{:S(2)}) %collective-permute-start.11) | collective-permute-done | bytes 262176 | tf_op jit(solution)/shard_map/ppermute | solution.py:31
  56.0 0.0 collective-permute-start.12
  56.0 2.8 %collective-permute-done.13.refs_6_ = bf16[32,4096]{1,0:T(8,128)(2,1)S(1)} collective-permute-done((bf16[32,4096]{1,0:T(8,128)(2,1)S(1)}, bf16[32,4096]{1,0:T(8,128)(2,1)S(1)}, u32[]{:S(2)}, u32[]{:S(2)}) %collective-permute-start.13) | collective-permute-done | bytes 262176 | tf_op jit(solution)/shard_map/ppermute | solution.py:31
  58.8 6.3 %collective-permute-start.14 = (bf16[32,4096]{1,0:T(8,128)(2,1)S(1)}, bf16[32,4096]{1,0:T(8,128)(2,1)S(1)}, u32[]{:S(2)}, u32[]{:S(2)}) collective-permute-start(bf16[32,4096]{1,0:T(8,128)(2,1)S(1)} %collective-permute-done.13.refs_6_), channel_id=1, source_target_pairs={{0,1},{1,0},{2,3},{3,2},{4,5},{5,4},{6,7},{7,6},{8,9},{9,8},{10,11... | collective-permute-start | bytes 786440 | tf_op jit(solution)/shard_map/ppermute | solution.py:31
  65.0 0.1 pad_add_fusion.place_ref
  65.1 0.0 collective-permute-done.8.refs_1_
  65.1 0.0 collective-permute-done.10.refs_3_
  65.1 0.0 collective-permute-done.12.refs_5_
  65.1 1.1 %collective-permute-done.14.refs_7_ = bf16[32,4096]{1,0:T(8,128)(2,1)S(1)} collective-permute-done((bf16[32,4096]{1,0:T(8,128)(2,1)S(1)}, bf16[32,4096]{1,0:T(8,128)(2,1)S(1)}, u32[]{:S(2)}, u32[]{:S(2)}) %collective-permute-start.14) | collective-permute-done | bytes 262176 | tf_op jit(solution)/shard_map/ppermute | solution.py:31
  66.2 5.9 %shard_map.62 = bf16[256,8,128]{2,1,0:T(8,128)(2,1)} custom-call(s32[4]{0:T(128)S(1)} %pad_add_fusion.place_ref, bf16[32,4096]{1,0:T(8,128)(2,1)S(1)} %shard_map.59.earlier_ref.refs_0_, bf16[32,4096]{1,0:T(8,128)(2,1)S(1)} %collective-permute-done.8.refs_1_, bf16[32,4096]{1,0:T(8,128)(2,1)S(1)} %collective-permute-done.9.refs_2_, ...), custom_call_target="tpu_custom_call" | custom-call | flops 2684354560 | bytes 14680064 | tf_op jit(solution)/shard_map/pallas_call | solution.py:188
  (4 shorter events, 0.0 us)
Async XLA Ops:
  0.0 21.9 %copy-start.2 = (bf16[1,32,4096]{2,1,0:T(8,128)(2,1)S(1)}, bf16[1,32,4096]{2,1,0:T(8,128)(2,1)}, u32[]{:S(2)}) copy-start(bf16[1,32,4096]{2,1,0:T(8,128)(2,1)} %param.6) | copy-start | bytes 786436
  0.0 39.8 %copy-start = (bf16[1,4096,1,8,128]{4,3,2,1,0:T(8,128)(2,1)S(1)}, bf16[1,4096,1,8,128]{4,3,2,1,0:T(8,128)(2,1)}, u32[]{:S(2)}) copy-start(bf16[1,4096,1,8,128]{4,3,2,1,0:T(8,128)(2,1)} %param.8) | copy-start | bytes 25165828
  1.8 4.5 %collective-permute-start.5 = (bf16[32,4096]{1,0:T(8,128)(2,1)S(1)}, bf16[32,4096]{1,0:T(8,128)(2,1)S(1)}, u32[]{:S(2)}, u32[]{:S(2)}) collective-permute-start(bf16[32,4096]{1,0:T(8,128)(2,1)S(1)} %get-tuple-element.11), channel_id=1, source_target_pairs={{0,1},{1,0},{2,3},{3,2},{4,5},{5,4},{6,7},{7,6},{8,9},{9,8},{10,11... | collective-permute-start | bytes 786440 | tf_op jit(solution)/shard_map/ppermute | solution.py:31
  5.2 5.6 %collective-permute-start.1 = (bf16[32,4096]{1,0:T(8,128)(2,1)S(1)}, bf16[32,4096]{1,0:T(8,128)(2,1)S(1)}, u32[]{:S(2)}, u32[]{:S(2)}) collective-permute-start(bf16[32,4096]{1,0:T(8,128)(2,1)S(1)} %get-tuple-element.15), channel_id=1, source_target_pairs={{0,1},{1,0},{2,3},{3,2},{4,5},{5,4},{6,7},{7,6},{8,9},{9,8},{10,11... | collective-permute-start | bytes 786440 | tf_op jit(solution)/shard_map/ppermute | solution.py:31
  5.3 7.5 %collective-permute-start.4 = (bf16[32,4096]{1,0:T(8,128)(2,1)S(1)}, bf16[32,4096]{1,0:T(8,128)(2,1)S(1)}, u32[]{:S(2)}, u32[]{:S(2)}) collective-permute-start(bf16[32,4096]{1,0:T(8,128)(2,1)S(1)} %get-tuple-element.13), channel_id=1, source_target_pairs={{0,1},{1,0},{2,3},{3,2},{4,5},{5,4},{6,7},{7,6},{8,9},{9,8},{10,11... | collective-permute-start | bytes 786440 | tf_op jit(solution)/shard_map/ppermute | solution.py:31
  6.4 8.8 %collective-permute-start.6 = (bf16[32,4096]{1,0:T(8,128)(2,1)S(1)}, bf16[32,4096]{1,0:T(8,128)(2,1)S(1)}, u32[]{:S(2)}, u32[]{:S(2)}) collective-permute-start(bf16[32,4096]{1,0:T(8,128)(2,1)S(1)} %shard_map.57), channel_id=1, source_target_pairs={{0,2},{1,7},{2,0},{3,5},{4,6},{5,3},{6,4},{7,1},{8,10},{9,15},{10,... | collective-permute-start | bytes 786440 | tf_op jit(solution)/shard_map/ppermute | solution.py:31
  10.8 10.3 %collective-permute-start = (bf16[32,4096]{1,0:T(8,128)(2,1)S(1)}, bf16[32,4096]{1,0:T(8,128)(2,1)S(1)}, u32[]{:S(2)}, u32[]{:S(2)}) collective-permute-start(bf16[32,4096]{1,0:T(8,128)(2,1)S(1)} %get-tuple-element.17), channel_id=1, source_target_pairs={{0,1},{1,0},{2,3},{3,2},{4,5},{5,4},{6,7},{7,6},{8,9},{9,8},{10,11... | collective-permute-start | bytes 786440 | tf_op jit(solution)/shard_map/ppermute | solution.py:31
  10.8 28.2 %copy-start.3 = (f32[1,4096]{1,0:T(1,128)S(1)}, f32[1,4096]{1,0:T(1,128)}, u32[]{:S(2)}) copy-start(f32[1,4096]{1,0:T(1,128)} %gain_ref.1) | copy-start | bytes 49156
  10.9 11.1 %collective-permute-start.2 = (bf16[32,4096]{1,0:T(8,128)(2,1)S(1)}, bf16[32,4096]{1,0:T(8,128)(2,1)S(1)}, u32[]{:S(2)}, u32[]{:S(2)}) collective-permute-start(bf16[32,4096]{1,0:T(8,128)(2,1)S(1)} %shard_map.55), channel_id=1, source_target_pairs={{0,2},{1,7},{2,0},{3,5},{4,6},{5,3},{6,4},{7,1},{8,10},{9,15},{10,... | collective-permute-start | bytes 786440 | tf_op jit(solution)/shard_map/ppermute | solution.py:31
  15.3 24.4 %copy-start.1 = (bf16[1,4096,1,2,128]{4,3,2,1,0:T(2,128)(2,1)S(1)}, bf16[1,4096,1,2,128]{4,3,2,1,0:T(2,128)(2,1)}, u32[]{:S(2)}) copy-start(bf16[1,4096,1,2,128]{4,3,2,1,0:T(2,128)(2,1)} %param.9) | copy-start | bytes 6291460
  15.4 19.5 %collective-permute-start.7 = (bf16[32,4096]{1,0:T(8,128)(2,1)S(1)}, bf16[32,4096]{1,0:T(8,128)(2,1)S(1)}, u32[]{:S(2)}, u32[]{:S(2)}) collective-permute-start(bf16[32,4096]{1,0:T(8,128)(2,1)S(1)} %shard_map.58), channel_id=1, source_target_pairs={{0,14},{1,11},{2,12},{3,9},{4,10},{5,15},{6,8},{7,13},{8,22},{9,19... | collective-permute-start | bytes 786440 | tf_op jit(solution)/shard_map/ppermute | solution.py:33
  22.1 16.9 %collective-permute-start.3 = (bf16[32,4096]{1,0:T(8,128)(2,1)S(1)}, bf16[32,4096]{1,0:T(8,128)(2,1)S(1)}, u32[]{:S(2)}, u32[]{:S(2)}) collective-permute-start(bf16[32,4096]{1,0:T(8,128)(2,1)S(1)} %shard_map.56), channel_id=1, source_target_pairs={{0,8},{1,9},{2,10},{3,11},{4,12},{5,13},{6,14},{7,15},{8,16},{9,17... | collective-permute-start | bytes 786440 | tf_op jit(solution)/shard_map/ppermute | solution.py:33
  39.2 11.7 %collective-permute-start.9 = (bf16[32,4096]{1,0:T(8,128)(2,1)S(1)}, bf16[32,4096]{1,0:T(8,128)(2,1)S(1)}, u32[]{:S(2)}, u32[]{:S(2)}) collective-permute-start(bf16[32,4096]{1,0:T(8,128)(2,1)S(1)} %shard_map.59.earlier_ref.refs_0_), channel_id=1, source_target_pairs={{0,6},{1,3},{2,4},{3,1},{4,2},{5,7},{6,0},{7,5},{8,14},{9,11},{10,... | collective-permute-start | bytes 786440 | tf_op jit(solution)/shard_map/ppermute | solution.py:31
  40.8 15.2 %collective-permute-start.11 = (bf16[32,4096]{1,0:T(8,128)(2,1)S(1)}, bf16[32,4096]{1,0:T(8,128)(2,1)S(1)}, u32[]{:S(2)}, u32[]{:S(2)}) collective-permute-start(bf16[32,4096]{1,0:T(8,128)(2,1)S(1)} %shard_map.61), channel_id=1, source_target_pairs={{0,2},{1,7},{2,0},{3,5},{4,6},{5,3},{6,4},{7,1},{8,10},{9,15},{10,... | collective-permute-start | bytes 786440 | tf_op jit(solution)/shard_map/ppermute | solution.py:31
  50.9 7.9 %collective-permute-start.13 = (bf16[32,4096]{1,0:T(8,128)(2,1)S(1)}, bf16[32,4096]{1,0:T(8,128)(2,1)S(1)}, u32[]{:S(2)}, u32[]{:S(2)}) collective-permute-start(bf16[32,4096]{1,0:T(8,128)(2,1)S(1)} %collective-permute-done.9.refs_2_), channel_id=1, source_target_pairs={{0,2},{1,7},{2,0},{3,5},{4,6},{5,3},{6,4},{7,1},{8,10},{9,15},{10,... | collective-permute-start | bytes 786440 | tf_op jit(solution)/shard_map/ppermute | solution.py:31
  50.9 14.3 %collective-permute-start.8 = (bf16[32,4096]{1,0:T(8,128)(2,1)S(1)}, bf16[32,4096]{1,0:T(8,128)(2,1)S(1)}, u32[]{:S(2)}, u32[]{:S(2)}) collective-permute-start(bf16[32,4096]{1,0:T(8,128)(2,1)S(1)} %shard_map.59.earlier_ref.refs_0_), channel_id=1, source_target_pairs={{0,1},{1,0},{2,3},{3,2},{4,5},{5,4},{6,7},{7,6},{8,9},{9,8},{10,11... | collective-permute-start | bytes 786440 | tf_op jit(solution)/shard_map/ppermute | solution.py:31
  55.0 10.2 %collective-permute-start.10 = (bf16[32,4096]{1,0:T(8,128)(2,1)S(1)}, bf16[32,4096]{1,0:T(8,128)(2,1)S(1)}, u32[]{:S(2)}, u32[]{:S(2)}) collective-permute-start(bf16[32,4096]{1,0:T(8,128)(2,1)S(1)} %collective-permute-done.9.refs_2_), channel_id=1, source_target_pairs={{0,1},{1,0},{2,3},{3,2},{4,5},{5,4},{6,7},{7,6},{8,9},{9,8},{10,11... | collective-permute-start | bytes 786440 | tf_op jit(solution)/shard_map/ppermute | solution.py:31
  56.0 9.1 %collective-permute-start.12 = (bf16[32,4096]{1,0:T(8,128)(2,1)S(1)}, bf16[32,4096]{1,0:T(8,128)(2,1)S(1)}, u32[]{:S(2)}, u32[]{:S(2)}) collective-permute-start(bf16[32,4096]{1,0:T(8,128)(2,1)S(1)} %collective-permute-done.11.refs_4_), channel_id=1, source_target_pairs={{0,1},{1,0},{2,3},{3,2},{4,5},{5,4},{6,7},{7,6},{8,9},{9,8},{10,11... | collective-permute-start | bytes 786440 | tf_op jit(solution)/shard_map/ppermute | solution.py:31
  58.8 7.4 %collective-permute-start.14 = (bf16[32,4096]{1,0:T(8,128)(2,1)S(1)}, bf16[32,4096]{1,0:T(8,128)(2,1)S(1)}, u32[]{:S(2)}, u32[]{:S(2)}) collective-permute-start(bf16[32,4096]{1,0:T(8,128)(2,1)S(1)} %collective-permute-done.13.refs_6_), channel_id=1, source_target_pairs={{0,1},{1,0},{2,3},{3,2},{4,5},{5,4},{6,7},{7,6},{8,9},{9,8},{10,11... | collective-permute-start | bytes 786440 | tf_op jit(solution)/shard_map/ppermute | solution.py:31
